TPU v7x, 128 devices: a whole 4x4x4 slice. The times are simulated.
128 devices in a mesh: row: 8 (over z, core), col: 16 (over x, y).
Axes of the slice: x: 4, y: 4, z: 4, core: 2. Of those that a mesh axis runs over, the one named last changes fastest.
Arguments:
- x_values: bfloat16 [1024, 12288], P('row', 'col'), may hold values from -6 to 6
- x_scales: bfloat16 [96, 1024], P('col', 'row'), may hold values from 0.25 to 4
- up_weight: bfloat16 [12288, 24576], P('col', 'row'), may hold values from -0.0546875 to 0.0546875
- down_weight: bfloat16 [24576, 12288], P('row', 'col'), may hold values from -0.0390625 to 0.0390625
- grad_values: bfloat16 [1024, 12288], P('row', 'col'), may hold values from -0.1875 to 0.1875
- grad_scales: bfloat16 [96, 1024], P('col', 'row'), may hold values from 0.25 to 4
Outputs:
- output: bfloat16 [1024, 12288], P('row', 'col')
- up_grad: float32 [12288, 24576], P('col', 'row')
All inputs are finite; a program needn't handle non-finite values.
Results may differ from a plain program's by a relative error of at most 0.039.
Values may be sent and summed in bfloat16 or wider, within the bound.
No kernel may reach another device: no remote copies, remote signals or barrier semaphores. Data moves between devices by JAX's collectives and lax.ppermute only.
A program may use at most 128 MiB of HBM per device.

v0:
```python
import functools

import jax
import jax.numpy as jnp
from jax import lax
from jax.experimental import pallas as pl
from jax.experimental.pallas import tpu as pltpu
from jax.sharding import PartitionSpec as P

BLOCK = 128
SIDE = 4
TILES = 6
BF16 = jnp.bfloat16
F32 = jnp.float32
COST = pl.CostEstimate(flops=1000, bytes_accessed=1000, transcendentals=0)


def gelu(v):
    return 0.5 * v * (1.0 + jnp.tanh(0.7978845608 * (v + 0.044715 * v * v * v)))


def gelu_slope(v):
    return jax.vjp(gelu, v)[1](jnp.ones_like(v))[0]


def scale_kernel(xv_ref, xs_ref, gv_ref, gs_ref, out_ref):
    n = xv_ref.shape[0]
    i = lax.broadcasted_iota(jnp.int32, (n, n), 0)
    diagonal = i == lax.broadcasted_iota(jnp.int32, (n, n), 1)
    for t, (values, scales) in enumerate(((xv_ref, xs_ref), (gv_ref, gs_ref))):
        for b in range(values.shape[1] // BLOCK):
            at = slice(b * BLOCK, (b + 1) * BLOCK)
            row = scales[b : b + 1, :].astype(F32)
            weight = jnp.where(diagonal, jnp.broadcast_to(row, (n, n)), 0.0).astype(BF16)
            block = jnp.dot(weight, values[:, at], preferred_element_type=F32)
            out_ref[t * n : (t + 1) * n, at] = block.astype(BF16)


def scaled(x_values, x_scales, grad_values, grad_scales):
    n, width = x_values.shape
    return pl.pallas_call(
        scale_kernel, out_shape=jax.ShapeDtypeStruct((2 * n, width), BF16), name="scale"
    )(x_values, x_scales, grad_values, grad_scales)


def share_dot(tensor, take, same_ref, other_ref, w_ref):
    width = same_ref.shape[-1]
    if tensor == 0:
        a = jnp.concatenate([r[...].reshape(-1, width) for r in (same_ref, other_ref)], axis=0)
    else:
        a = jnp.where(take == 0, same_ref[...], other_ref[...]).reshape(-1, width)
    dims = (((1,), (tensor,)), ((), ()))
    return lax.dot_general(a, w_ref[...], dims, preferred_element_type=F32)


def core_of(slot_ref, step):
    return lax.div(lax.rem(slot_ref[0] + step, SIDE), 2)


def far_kernel(tensor, slot_ref, same_ref, other_ref, w_ref, low_ref, high_ref):
    j, half = pl.program_id(0), pl.num_programs(0) // 2
    out = share_dot(tensor, core_of(slot_ref, 2), same_ref, other_ref, w_ref).astype(BF16)

    @pl.when(j < half)
    def _():
        low_ref[...] = out

    @pl.when(j >= half)
    def _():
        high_ref[...] = out


def near_kernel(tensor, slot_ref, *refs):
    w_ref, outs = refs[6], refs[7:]
    for i, step in enumerate((1, 3, 0)):
        same_ref, other_ref = refs[2 * i : 2 * i + 2]
        out = share_dot(tensor, core_of(slot_ref, step), same_ref, other_ref, w_ref)
        outs[i][...] = out.astype(BF16)


def add_kernel(slot_ref, after_ref, before_ref, low_ref, high_ref, after_out, before_out):
    after_out[...] = (after_ref[...].astype(F32) + low_ref[...].astype(F32)).astype(BF16)
    before_out[...] = (before_ref[...].astype(F32) + high_ref[...].astype(F32)).astype(BF16)


def blocks_kernel(slots_ref, a_ref, b_ref, c_ref, *outs):
    total = sum(r[...].astype(F32) for r in (a_ref, b_ref, c_ref))
    for i, out in enumerate(outs):

        @pl.when(pl.program_id(0) == i)
        def _():
            out[...] = total.astype(out.dtype)


def row_blocks(terms, place):
    big, units = terms[0].shape
    small = big // SIDE
    slots = lax.rem(place + jnp.array([2, 1, 3, 0], jnp.int32), SIDE)
    grid = pltpu.PrefetchScalarGridSpec(
        num_scalar_prefetch=1,
        grid=(SIDE,),
        in_specs=[pl.BlockSpec((small, units), lambda j, slots: (slots[j], 0))] * 3,
        out_specs=[pl.BlockSpec((small, units), lambda j, slots: (0, 0))] * 4,
    )
    return pl.pallas_call(
        blocks_kernel,
        grid_spec=grid,
        out_shape=[pltpu.HBM((small, units), kind) for kind in (BF16, BF16, BF16, F32)],
        cost_estimate=COST,
        name="row_blocks",
    )(slots, *terms)


def act_kernel(a_ref, b_ref, c_ref, d_ref, pre_ref, hidden_ref):
    pre = a_ref[...] + sum(r[...].astype(F32) for r in (b_ref, c_ref, d_ref))
    pre_ref[...] = pre
    hidden_ref[...] = gelu(pre).astype(BF16)


def slope_kernel(a_ref, b_ref, c_ref, d_ref, pre_ref, out_ref):
    grad = a_ref[...] + sum(r[...].astype(F32) for r in (b_ref, c_ref, d_ref))
    out_ref[...] = (grad * gelu_slope(pre_ref[...])).astype(BF16)


def by_tiles(kernel, ins, kinds, name):
    rows_in, units = ins[0].shape
    spec = pl.BlockSpec((rows_in, units // 3), lambda j: (0, j))
    return pl.pallas_call(
        kernel,
        grid=(3,),
        in_specs=[spec] * len(ins),
        out_specs=[spec] * len(kinds),
        out_shape=[jax.ShapeDtypeStruct((rows_in, units), kind) for kind in kinds],
        cost_estimate=COST,
        name=name,
    )(*ins)


def put_kernel(slot_ref, mine_ref, far_ref, before_ref, after_ref, out_ref):
    small = mine_ref.shape[0]
    for step, block in ((0, mine_ref), (2, far_ref), (3, before_ref), (1, after_ref)):
        at = pl.multiple_of(lax.rem(slot_ref[0] + step, SIDE) * small, small)
        out_ref[pl.ds(at, small), :] = block[...]


def in_order(blocks, place):
    small, units = blocks[0].shape
    tile = units // 3
    grid = pltpu.PrefetchScalarGridSpec(
        num_scalar_prefetch=1,
        grid=(3,),
        in_specs=[pl.BlockSpec((small, tile), lambda j, slot: (0, j))] * 4,
        out_specs=pl.BlockSpec((SIDE * small, tile), lambda j, slot: (0, j)),
    )
    return pl.pallas_call(
        put_kernel,
        grid_spec=grid,
        out_shape=jax.ShapeDtypeStruct((SIDE * small, units), BF16),
        cost_estimate=COST,
        name="in_order",
    )(place.reshape(1), *blocks)


def in_hbm(a):
    return pltpu.with_memory_space_constraint(a, pltpu.HBM)


class Shares:
    def __init__(self, tensor, held, weight):
        self.tensor, self.weight = tensor, weight
        self.small, self.width = held[0].shape[3:]
        self.units = weight.shape[1 - tensor]
        self.tile = self.units // TILES
        self.big = SIDE * self.small

    def rows_spec(self, step):
        def along_x(j, slot):
            return (lax.rem(slot[0] + step, SIDE), 0, 0, 0, 0)

        def along_y(j, slot):
            return (0, 1, lax.rem(lax.rem(slot[0] + step, SIDE), 2), 0, 0)

        if self.tensor == 0:
            return pl.BlockSpec((1, 1, 2, self.small, self.width), along_x)
        return pl.BlockSpec((SIDE, 1, 1, self.small, self.width), along_y)

    def weight_spec(self):
        if self.tensor == 0:
            return pl.BlockSpec((self.width, self.tile), lambda j, slot: (0, j))
        return pl.BlockSpec((self.tile, self.width), lambda j, slot: (j, 0))

    def call(self, kernel, place, held, steps, outs, specs, name):
        grid = pltpu.PrefetchScalarGridSpec(
            num_scalar_prefetch=1,
            grid=(TILES,),
            in_specs=[self.rows_spec(step) for step in steps for _ in held] + [self.weight_spec()],
            out_specs=specs,
        )
        return pl.pallas_call(
            functools.partial(kernel, self.tensor),
            grid_spec=grid,
            out_shape=outs,
            compiler_params=pltpu.CompilerParams(vmem_limit_bytes=24 * 1024 * 1024),
            cost_estimate=COST,
            name=name,
        )(place.reshape(1), *(held * len(steps)), in_hbm(self.weight))

    def far(self, place, held):
        half = jax.ShapeDtypeStruct((self.big, self.units // 2), BF16)
        last = TILES // 2 - 1
        shape = (self.big, self.tile)
        specs = [
            pl.BlockSpec(shape, lambda j, slot: (0, jnp.minimum(j, last))),
            pl.BlockSpec(shape, lambda j, slot: (0, jnp.maximum(j - last - 1, 0))),
        ]
        return self.call(far_kernel, place, held, (2,), [half, half], specs, "far_share")

    def near(self, place, held):
        whole = (self.big, self.units)
        outs = [pltpu.HBM(whole, BF16)] * 3
        specs = [pl.BlockSpec((self.big, self.tile), lambda j, slot: (0, j))] * 3
        return self.call(near_kernel, place, held, (1, 3, 0), outs, specs, "near_shares")

    def add(self, place, after, before, got):
        block = (self.big, self.tile)
        first = pl.BlockSpec(block, lambda j, slot: (0, j))
        second = pl.BlockSpec(block, lambda j, slot: (0, j + TILES // 2))
        grid = pltpu.PrefetchScalarGridSpec(
            num_scalar_prefetch=1,
            grid=(TILES // 2,),
            in_specs=[first, second, first, first],
            out_specs=[first, second],
        )
        return pl.pallas_call(
            add_kernel,
            grid_spec=grid,
            out_shape=[pltpu.HBM(after.shape, BF16)] * 2,
            input_output_aliases={1: 0, 2: 1},
            cost_estimate=COST,
            name="add_far",
        )(place.reshape(1), in_hbm(after), in_hbm(before), *got)


def steps_on(axis, step):
    if axis == "x":
        return [(4 * x + y, 4 * ((x + step) % 4) + y) for x in range(4) for y in range(4)]
    if axis == "y":
        return [(4 * x + y, 4 * x + (y + step) % 4) for x in range(4) for y in range(4)]
    if axis == "z":
        return [(2 * z + c, 2 * ((z + step) % 4) + c) for z in range(4) for c in range(2)]
    return [(r, r ^ 1) for r in range(8)]


def send(a, axis, step):
    return lax.ppermute(a, "col" if axis in ("x", "y") else "row", steps_on(axis, step))


def trade(*sends):
    held = lax.optimization_barrier([a for a, _, _ in sends])
    return [send(a, axis, step) for a, (_, axis, step) in zip(held, sends)]


def gate(value, *earlier):
    return lax.optimization_barrier((value, earlier))[0]


def wide_gather(mine, place, axis):
    n = mine.shape[0] // 2
    before, after = trade((mine, axis, 1), (mine, axis, -1))
    far = trade((before[:n], axis, 1), (after[n:], axis, -1))
    return [
        (place, 0, mine),
        (place + 3, 0, before),
        (place + 1, 0, after),
        (place + 2, 0, far[0]),
        (place + 2, n, far[1]),
    ]


def local(x_values, x_scales, up_weight, down_weight, grad_values, grad_scales):
    col = lax.axis_index("col")
    x, y = col // SIDE, lax.rem(col, SIDE)
    n, width = x_values.shape
    small, tokens, units = n // 2, 8 * n, up_weight.shape[1]
    big, cut = tokens // SIDE, units // 2

    own = scaled(x_values, x_scales, grad_values, grad_scales)
    far, above, below = trade((own, "z", 2), (own, "z", -1), (own, "z", 1))
    same = jnp.concatenate([own, above, far, below], axis=0)
    held = [a.reshape(SIDE, 2, 2, small, width) for a in (same, send(same, "core", 1))]
    up, down = Shares(0, held, up_weight), Shares(1, held, down_weight)
    x_far = up.far(x, held)
    x_got = trade((x_far[0], "x", 1), (x_far[1], "x", -1))
    g_far = down.far(gate(y, x_far[0]), held)
    g_got = trade((g_far[0], "y", 1), (g_far[1], "y", -1))
    *x_near, x_mine = up.near(gate(x, g_far[0]), held)
    *g_near, g_mine = down.near(gate(y, x_mine), held)
    x_near = up.add(gate(x, g_mine), *x_near, x_got)
    x_got = trade((x_near[0], "x", 1), (x_near[1], "x", -1))
    g_near = down.add(gate(y, x_near[0]), *g_near, g_got)
    g_got = trade((g_near[0], "y", 1), (g_near[1], "y", -1))
    crossed = jnp.stack(held)[:, :, 0].transpose(0, 2, 1, 3, 4).reshape(tokens, width)

    def narrow(terms, place, axis):
        far, after, before, mine = row_blocks(terms, place)
        return [mine] + trade((far, axis, 2), (after, axis, 1), (before, axis, -1))

    def gather_narrow(mine, place, axis):
        got = trade((mine, axis, 2), (mine, axis, 1), (mine, axis, -1))
        return in_order([mine] + got, place)

    pre, hidden = by_tiles(act_kernel, narrow([x_mine] + x_got, y, "y"), (F32, BF16), "act")
    grad = narrow([g_mine] + g_got, x, "x")
    (grad_pre,) = by_tiles(slope_kernel, grad + [pre], (BF16,), "slope")
    hidden = wide_gather(gather_narrow(hidden, y, "y"), x, "x")
    grad_pre = wide_gather(gather_narrow(grad_pre, x, "x"), y, "y")

    terms = jnp.zeros((tokens, width), F32)
    for slot, ahead, block in hidden:
        term = jnp.dot(block, down_weight, preferred_element_type=F32)
        terms = lax.dynamic_update_slice_in_dim(terms, term, lax.rem(slot, SIDE) * big + ahead, 0)
    terms = terms.reshape(SIDE, 2, n, width)
    other = send(terms[:, 1].astype(BF16).reshape(tokens // 2, width), "core", 1)
    mine = terms[:, 0] + other.astype(F32).reshape(SIDE, n, width)
    sends = mine.astype(BF16)
    got = trade((sends[2], "z", 2), (sends[1], "z", 1), (sends[3], "z", -1))
    output = mine[0] + got[0].astype(F32) + got[1].astype(F32) + got[2].astype(F32)

    whole = jnp.zeros((tokens, units), BF16)
    for slot, ahead, block in grad_pre:
        whole = lax.dynamic_update_slice_in_dim(whole, block, lax.rem(slot, SIDE) * big + ahead, 0)
    up_grad = lax.dot_general(
        crossed, whole, (((0,), (0,)), ((), ())), preferred_element_type=F32
    )
    return (output.astype(BF16), up_grad)


def solution(mesh):
    placed = (
        P("row", "col"),
        P("col", "row"),
        P("col", "row"),
        P("row", "col"),
        P("row", "col"),
        P("col", "row"),
    )
    return jax.shard_map(
        local,
        mesh=mesh,
        in_specs=placed,
        out_specs=(P("row", "col"), P("col", "row")),
        check_vma=False,
    )
```

profile of v0, /device:TPU:0, one launch (start us, length us, event | category | flops | bytes accessed | tf_op | source)
XLA Modules:
  0.0 242.5 jit_solution(13391398950218534956)
XLA Ops:
  0.6 2.0 scale.1
  2.7 2.0 collective-permute-start.2
  4.7 3.6 %collective-permute-start.1 = (bf16[256,768]{1,0:T(8,128)(2,1)}, bf16[256,768]{1,0:T(8,128)(2,1)S(1)}, u32[]{:S(2)}, u32[]{:S(2)}) collective-permute-start(bf16[256,768]{1,0:T(8,128)(2,1)} %scale.1), channel_id=1, source_target_pairs={{0,64},{16,80},{32,96},{48,112},{64,0},{80,16},{96,32},{112,48},{1... | collective-permute-start | bytes 1179656 | tf_op jit(solution)/shard_map/ppermute | solution.py:255
  8.3 1.0 collective-permute-start
  9.3 6.9 %collective-permute-done.2 = bf16[256,768]{1,0:T(8,128)(2,1)S(1)} collective-permute-done((bf16[256,768]{1,0:T(8,128)(2,1)}, bf16[256,768]{1,0:T(8,128)(2,1)S(1)}, u32[]{:S(2)}, u32[]{:S(2)}) %collective-permute-start.2) | collective-permute-done | bytes 393248 | tf_op jit(solution)/shard_map/ppermute | solution.py:255
  16.1 9.6 %collective-permute-done.1 = bf16[256,768]{1,0:T(8,128)(2,1)S(1)} collective-permute-done((bf16[256,768]{1,0:T(8,128)(2,1)}, bf16[256,768]{1,0:T(8,128)(2,1)S(1)}, u32[]{:S(2)}, u32[]{:S(2)}) %collective-permute-start.1) | collective-permute-done | bytes 393248 | tf_op jit(solution)/shard_map/ppermute | solution.py:255
  25.7 1.1 pad_maximum_fusion.1
  26.9 3.4 %collective-permute-done.3 = bf16[1024,768]{1,0:T(8,128)(2,1)S(1)} collective-permute-done((bf16[1024,768]{1,0:T(8,128)(2,1)S(1)}, bf16[1024,768]{1,0:T(8,128)(2,1)S(1)}, u32[]{:S(2)}, u32[]{:S(2)}) %collective-permute-start.3) | collective-permute-done | bytes 1572896 | tf_op jit(solution)/shard_map/ppermute | solution.py:255
  30.3 5.3 %far_share.2 = (bf16[256,1536]{1,0:T(8,128)(2,1)S(1)}, bf16[256,1536]{1,0:T(8,128)(2,1)S(1)}) custom-call(s32[1]{0:T(128)} %bitcast.6.slot_ref, bf16[4,2,2,64,768]{4,3,2,1,0:T(8,128)(2,1)S(1)} %bitcast.52, bf16[4,2,2,64,768]{4,3,2,1,0:T(8,128)(2,1)S(1)} %bitcast.61, bf16[768,3072]{1,0:T(8,128)(2,1)} %w_ref.2), custom_call_target="tpu_custom_call" | custom-call | flops 1000 | bytes 1000 | tf_op jit(solution)/shard_map/far_share/pallas_call | solution.py:199
  35.6 1.6 collective-permute-start.4
  37.2 1.7 collective-permute-start.5
  38.9 6.5 %far_share.3 = (bf16[256,1536]{1,0:T(8,128)(2,1)}, bf16[256,1536]{1,0:T(8,128)(2,1)}) custom-call(s32[1]{0:T(128)} %bitcast.20.slot_ref, bf16[4,2,2,64,768]{4,3,2,1,0:T(8,128)(2,1)S(1)} %bitcast.53, bf16[4,2,2,64,768]{4,3,2,1,0:T(8,128)(2,1)S(1)} %bitcast.62, bf16[3072,768]{1,0:T(8,128)(2,1)} %w_ref.3), custom_call_target="tpu_custom_call" | custom-call | flops 1000 | bytes 1000 | tf_op jit(solution)/shard_map/far_share/pallas_call | solution.py:199
  45.5 1.6 collective-permute-start.22
  47.1 1.7 collective-permute-start.23
  48.7 7.6 %near_shares.2 = (bf16[256,3072]{1,0:T(8,128)(2,1)}, bf16[256,3072]{1,0:T(8,128)(2,1)}, bf16[256,3072]{1,0:T(8,128)(2,1)}) custom-call(s32[1]{0:T(128)} %bitcast.1.slot_ref, bf16[4,2,2,64,768]{4,3,2,1,0:T(8,128)(2,1)S(1)} %bitcast.54, bf16[4,2,2,64,768]{4,3,2,1,0:T(8,128)(2,1)S(1)} %bitcast.63, bf16[4,2,2,64,768]{4,3,2,1,0:T(8,128)(2,1)S(1)} %bitcast.55, ...), custom_call_target="tpu_custom_call" | custom-call | flops 1000 | bytes 1000 | tf_op jit(solution)/shard_map/near_shares/pallas_call | solution.py:199
  56.3 7.9 %near_shares.3 = (bf16[256,3072]{1,0:T(8,128)(2,1)}, bf16[256,3072]{1,0:T(8,128)(2,1)}, bf16[256,3072]{1,0:T(8,128)(2,1)}) custom-call(s32[1]{0:T(128)} %bitcast.4.slot_ref, bf16[4,2,2,64,768]{4,3,2,1,0:T(8,128)(2,1)S(1)} %bitcast.57, bf16[4,2,2,64,768]{4,3,2,1,0:T(8,128)(2,1)S(1)} %bitcast.66, bf16[4,2,2,64,768]{4,3,2,1,0:T(8,128)(2,1)S(1)} %bitcast.58, ...), custom_call_target="tpu_custom_call" | custom-call | flops 1000 | bytes 1000 | tf_op jit(solution)/shard_map/near_shares/pallas_call | solution.py:199
  64.2 0.9 copy-done.2
  65.1 1.0 copy-done.3
  66.1 3.8 %add_far.2 = (bf16[256,3072]{1,0:T(8,128)(2,1)}, bf16[256,3072]{1,0:T(8,128)(2,1)}) custom-call(s32[1]{0:T(128)} %bitcast.5.slot_ref, bf16[256,3072]{1,0:T(8,128)(2,1)} %get-tuple-element.61.after_ref, bf16[256,3072]{1,0:T(8,128)(2,1)} %get-tuple-element.62.before_ref, bf16[256,1536]{1,0:T(8,128)(2,1)} %copy-done.2, ...), custom_call_target="tpu_custom_call", output_to_operand_aliasing={{0}: (1, {}), {1}: (2, {})} | custom-call | flops 1000 | bytes 1000 | tf_op jit(solution)/shard_map/add_far/pallas_call | solution.py:234
  70.1 3.0 %collective-permute-start.7 = (bf16[256,3072]{1,0:T(8,128)(2,1)}, bf16[256,3072]{1,0:T(8,128)(2,1)}, u32[]{:S(2)}, u32[]{:S(2)}) collective-permute-start(bf16[256,3072]{1,0:T(8,128)(2,1)} %get-tuple-element.66), channel_id=1, source_target_pairs={{0,12},{1,13},{2,14},{3,15},{4,0},{5,1},{6,2},{7,3},{8,4},{9,5},{1... | collective-permute-start | bytes 4718600 | tf_op jit(solution)/shard_map/ppermute | solution.py:255
  73.1 3.8 %add_far.3 = (bf16[256,3072]{1,0:T(8,128)(2,1)}, bf16[256,3072]{1,0:T(8,128)(2,1)}) custom-call(s32[1]{0:T(128)} %bitcast.20.slot_ref, bf16[256,3072]{1,0:T(8,128)(2,1)} %get-tuple-element.85.after_ref, bf16[256,3072]{1,0:T(8,128)(2,1)} %get-tuple-element.86.before_ref, ...), custom_call_target="tpu_custom_call", output_to_operand_aliasing={{0}: (1, {}), {1}: (2, {})} | custom-call | flops 1000 | bytes 1000 | tf_op jit(solution)/shard_map/add_far/pallas_call | solution.py:234
  77.3 2.9 %collective-permute-start.25 = (bf16[256,3072]{1,0:T(8,128)(2,1)}, bf16[256,3072]{1,0:T(8,128)(2,1)}, u32[]{:S(2)}, u32[]{:S(2)}) collective-permute-start(bf16[256,3072]{1,0:T(8,128)(2,1)} %get-tuple-element.90), channel_id=1, source_target_pairs={{0,3},{1,0},{2,1},{3,2},{4,7},{5,4},{6,5},{7,6},{8,11},{9,8},{10,9... | collective-permute-start | bytes 4718600 | tf_op jit(solution)/shard_map/ppermute | solution.py:255
  80.7 26.0 %collective-permute-done.6.b_ref = bf16[256,3072]{1,0:T(8,128)(2,1)} collective-permute-done((bf16[256,3072]{1,0:T(8,128)(2,1)}, bf16[256,3072]{1,0:T(8,128)(2,1)}, u32[]{:S(2)}, u32[]{:S(2)}) %collective-permute-start.6) | collective-permute-done | bytes 1572896 | tf_op jit(solution)/shard_map/ppermute | solution.py:255
  106.8 5.5 %row_blocks.2 = (bf16[64,3072]{1,0:T(8,128)(2,1)}, bf16[64,3072]{1,0:T(8,128)(2,1)}, bf16[64,3072]{1,0:T(8,128)(2,1)}, f32[64,3072]{1,0:T(8,128)}) custom-call(s32[4]{0:T(128)} %get-tuple-element.112.slots_ref, bf16[256,3072]{1,0:T(8,128)(2,1)} %get-tuple-element.57.a_ref, bf16[256,3072]{1,0:T(8,128)(2,1)} %collective-permute-done.6.b_ref, ...), custom_call_target="tpu_custom_call" | custom-call | flops 1000 | bytes 1000 | tf_op jit(solution)/shard_map/row_blocks/pallas_call | solution.py:105
  112.2 1.9 collective-permute-start.8
  114.8 2.6 %collective-permute-start.10 = (bf16[64,3072]{1,0:T(8,128)(2,1)}, bf16[64,3072]{1,0:T(8,128)(2,1)}, u32[]{:S(2)}, u32[]{:S(2)}) collective-permute-start(bf16[64,3072]{1,0:T(8,128)(2,1)} %get-tuple-element.73), channel_id=1, source_target_pairs={{0,3},{1,0},{2,1},{3,2},{4,7},{5,4},{6,5},{7,6},{8,11},{9,8},{10,9... | collective-permute-start | bytes 1179656 | tf_op jit(solution)/shard_map/ppermute | solution.py:255
  117.4 5.5 %row_blocks.3 = (bf16[64,3072]{1,0:T(8,128)(2,1)}, bf16[64,3072]{1,0:T(8,128)(2,1)}, bf16[64,3072]{1,0:T(8,128)(2,1)}, f32[64,3072]{1,0:T(8,128)}) custom-call(s32[4]{0:T(128)} %get-tuple-element.111.slots_ref, bf16[256,3072]{1,0:T(8,128)(2,1)} %get-tuple-element.59.a_ref, bf16[256,3072]{1,0:T(8,128)(2,1)} %collective-permute-done.24.b_ref, ...), custom_call_target="tpu_custom_call" | custom-call | flops 1000 | bytes 1000 | tf_op jit(solution)/shard_map/row_blocks/pallas_call | solution.py:105
  122.9 1.5 collective-permute-start.26
  124.4 2.3 collective-permute-start.27
  126.7 2.4 collective-permute-start.28
  129.1 2.6 %collective-permute-done.9.c_ref = bf16[64,3072]{1,0:T(8,128)(2,1)} collective-permute-done((bf16[64,3072]{1,0:T(8,128)(2,1)}, bf16[64,3072]{1,0:T(8,128)(2,1)}, u32[]{:S(2)}, u32[]{:S(2)}) %collective-permute-start.9) | collective-permute-done | bytes 393248 | tf_op jit(solution)/shard_map/ppermute | solution.py:255
  131.6 3.4 %act.1 = (f32[64,3072]{1,0:T(8,128)}, bf16[64,3072]{1,0:T(8,128)(2,1)}) custom-call(f32[64,3072]{1,0:T(8,128)} %get-tuple-element.67.a_ref, bf16[64,3072]{1,0:T(8,128)(2,1)} %collective-permute-done.8.b_ref, bf16[64,3072]{1,0:T(8,128)(2,1)} %collective-permute-done.9.c_ref, bf16[64,3072]{1,0:T(8,128)(2,1)} %collective-permute-done.10.d_ref), custom_call_target="tpu_custom_call" | custom-call | flops 1000 | bytes 1000 | tf_op jit(solution)/shard_map/act/pallas_call | solution.py:128
  135.0 1.7 collective-permute-start.11
  137.6 2.5 %collective-permute-start.13 = (bf16[64,3072]{1,0:T(8,128)(2,1)}, bf16[64,3072]{1,0:T(8,128)(2,1)}, u32[]{:S(2)}, u32[]{:S(2)}) collective-permute-start(bf16[64,3072]{1,0:T(8,128)(2,1)} %get-tuple-element.77.mine_ref), channel_id=1, source_target_pairs={{0,3},{1,0},{2,1},{3,2},{4,7},{5,4},{6,5},{7,6},{8,11},{9,8},{10,9... | collective-permute-start | bytes 1179656 | tf_op jit(solution)/shard_map/ppermute | solution.py:255
  140.0 1.4 collective-permute-done.27.c_ref
  141.4 3.7 %slope.1.mine_ref = bf16[64,3072]{1,0:T(8,128)(2,1)} custom-call(f32[64,3072]{1,0:T(8,128)} %get-tuple-element.91.a_ref, bf16[64,3072]{1,0:T(8,128)(2,1)} %copy-done.4, bf16[64,3072]{1,0:T(8,128)(2,1)} %collective-permute-done.27.c_ref, bf16[64,3072]{1,0:T(8,128)(2,1)} %collective-permute-done.28.d_ref, f32[64,3072]{1,0:T(8,128)} %get-tuple-element.98.pre_ref), custom_call_target="tpu_custom_call" | custom-call | flops 1000 | bytes 1000 | tf_op jit(solution)/shard_map/slope/pallas_call | solution.py:128
  145.1 1.2 collective-permute-start.29
  146.3 2.3 collective-permute-start.30
  148.9 2.7 %collective-permute-start.31 = (bf16[64,3072]{1,0:T(8,128)(2,1)}, bf16[64,3072]{1,0:T(8,128)(2,1)}, u32[]{:S(2)}, u32[]{:S(2)}) collective-permute-start(bf16[64,3072]{1,0:T(8,128)(2,1)} %slope.1.mine_ref), channel_id=1, source_target_pairs={{0,12},{1,13},{2,14},{3,15},{4,0},{5,1},{6,2},{7,3},{8,4},{9,5},{1... | collective-permute-start | bytes 1179656 | tf_op jit(solution)/shard_map/ppermute | solution.py:255
  151.6 4.8 %collective-permute-done.12.before_ref = bf16[64,3072]{1,0:T(8,128)(2,1)} collective-permute-done((bf16[64,3072]{1,0:T(8,128)(2,1)}, bf16[64,3072]{1,0:T(8,128)(2,1)}, u32[]{:S(2)}, u32[]{:S(2)}) %collective-permute-start.12) | collective-permute-done | bytes 393248 | tf_op jit(solution)/shard_map/ppermute | solution.py:255
  156.3 3.4 %in_order.2 = bf16[256,3072]{1,0:T(8,128)(2,1)} custom-call(s32[1]{0:T(128)} %bitcast.slot_ref, bf16[64,3072]{1,0:T(8,128)(2,1)} %get-tuple-element.77.mine_ref, bf16[64,3072]{1,0:T(8,128)(2,1)} %collective-permute-done.11.far_ref, bf16[64,3072]{1,0:T(8,128)(2,1)} %collective-permute-done.12.before_ref, bf16[64,3072]{1,0:T(8,128)(2,1)} %collective-permute-done.13.after_ref), custom_call_target="tpu_custom_call" | custom-call | flops 1000 | bytes 1000 | tf_op jit(solution)/shard_map/in_order/pallas_call | solution.py:155
  159.8 3.2 %collective-permute-start.15 = (bf16[256,3072]{1,0:T(8,128)(2,1)}, bf16[256,3072]{1,0:T(8,128)(2,1)}, u32[]{:S(2)}, u32[]{:S(2)}) collective-permute-start(bf16[256,3072]{1,0:T(8,128)(2,1)} %in_order.2), channel_id=1, source_target_pairs={{0,12},{1,13},{2,14},{3,15},{4,0},{5,1},{6,2},{7,3},{8,4},{9,5},{1... | collective-permute-start | bytes 4718600 | tf_op jit(solution)/shard_map/ppermute | solution.py:255
  163.0 3.4 %collective-permute-done.30.before_ref = bf16[64,3072]{1,0:T(8,128)(2,1)} collective-permute-done((bf16[64,3072]{1,0:T(8,128)(2,1)}, bf16[64,3072]{1,0:T(8,128)(2,1)}, u32[]{:S(2)}, u32[]{:S(2)}) %collective-permute-start.30) | collective-permute-done | bytes 393248 | tf_op jit(solution)/shard_map/ppermute | solution.py:255
  166.4 1.0 collective-permute-done.31.after_ref
  167.4 3.5 %in_order.3 = bf16[256,3072]{1,0:T(8,128)(2,1)} custom-call(s32[1]{0:T(128)} %bitcast.6.slot_ref, bf16[64,3072]{1,0:T(8,128)(2,1)} %slope.1.mine_ref, bf16[64,3072]{1,0:T(8,128)(2,1)} %copy-done.5, bf16[64,3072]{1,0:T(8,128)(2,1)} %collective-permute-done.30.before_ref, bf16[64,3072]{1,0:T(8,128)(2,1)} %collective-permute-done.31.after_ref), custom_call_target="tpu_custom_call" | custom-call | flops 1000 | bytes 1000 | tf_op jit(solution)/shard_map/in_order/pallas_call | solution.py:155
  170.9 3.2 %collective-permute-start.33 = (bf16[256,3072]{1,0:T(8,128)(2,1)}, bf16[256,3072]{1,0:T(8,128)(2,1)}, u32[]{:S(2)}, u32[]{:S(2)}) collective-permute-start(bf16[256,3072]{1,0:T(8,128)(2,1)} %in_order.3), channel_id=1, source_target_pairs={{0,3},{1,0},{2,1},{3,2},{4,7},{5,4},{6,5},{7,6},{8,11},{9,8},{10,9... | collective-permute-start | bytes 4718600 | tf_op jit(solution)/shard_map/ppermute | solution.py:255
  177.9 1.4 convolution_dynamic-update-slice_fusion.2
  179.3 20.7 %collective-permute-done.14 = bf16[256,3072]{1,0:T(8,128)(2,1)} collective-permute-done((bf16[256,3072]{1,0:T(8,128)(2,1)}, bf16[256,3072]{1,0:T(8,128)(2,1)}, u32[]{:S(2)}, u32[]{:S(2)}) %collective-permute-start.14) | collective-permute-done | bytes 1572896 | tf_op jit(solution)/shard_map/ppermute | solution.py:255
  200.0 1.2 slice.45
  201.2 1.2 slice.46
  202.5 3.2 %collective-permute-start.17 = (bf16[128,3072]{1,0:T(8,128)(2,1)S(1)}, bf16[128,3072]{1,0:T(8,128)(2,1)S(1)}, u32[]{:S(2)}, u32[]{:S(2)}) collective-permute-start(bf16[128,3072]{1,0:T(8,128)(2,1)S(1)} %slice.46), channel_id=1, source_target_pairs={{0,12},{1,13},{2,14},{3,15},{4,0},{5,1},{6,2},{7,3},{8,4},{9,5},{1... | collective-permute-start | bytes 2359304 | tf_op jit(solution)/shard_map/ppermute | solution.py:255
  205.7 2.0 collective-permute-done.32
  207.7 1.2 slice.53
  208.9 1.2 slice.54
  210.2 3.2 %collective-permute-start.35 = (bf16[128,3072]{1,0:T(8,128)(2,1)S(1)}, bf16[128,3072]{1,0:T(8,128)(2,1)S(1)}, u32[]{:S(2)}, u32[]{:S(2)}) collective-permute-start(bf16[128,3072]{1,0:T(8,128)(2,1)S(1)} %slice.54), channel_id=1, source_target_pairs={{0,3},{1,0},{2,1},{3,2},{4,7},{5,4},{6,5},{7,6},{8,11},{9,8},{10,9... | collective-permute-start | bytes 2359304 | tf_op jit(solution)/shard_map/ppermute | solution.py:255
  213.4 2.9 %convolution_dynamic-update-slice_fusion.1 = f32[1024,768]{1,0:T(8,128)S(1)} fusion(f32[1024,768]{1,0:T(8,128)S(1)} %convolution_dynamic-update-slice_fusion.2, s32[]{:T(128)S(6)} %select_n.37, bf16[256,3072]{1,0:T(8,128)(2,1)} %collective-permute-done.14, bf16[3072,768]{1,0:T(8,128)(2,1)S(1)} %bitcast.71), kind=kOutput, calls=%fused_computation.6 | convolution fusion | flops 1207959552 | bytes 7077892 | tf_op jit(solution)/shard_map/dot_general | solution.py:320
  216.2 2.9 %convolution_dynamic-update-slice_fusion = f32[1024,768]{1,0:T(8,128)S(1)} fusion(f32[1024,768]{1,0:T(8,128)S(1)} %convolution_dynamic-update-slice_fusion.1, s32[]{:T(128)S(6)} %select_n.38, bf16[256,3072]{1,0:T(8,128)(2,1)} %collective-permute-done.15, bf16[3072,768]{1,0:T(8,128)(2,1)S(1)} %bitcast.71), kind=kOutput, calls=%fused_computation.5 | convolution fusion | flops 1207959552 | bytes 7077892 | tf_op jit(solution)/shard_map/dot_general | solution.py:320
  219.1 1.6 constant_dynamic-update-slice_fusion.3
  220.7 2.5 %collective-permute-done.16 = bf16[128,3072]{1,0:T(8,128)(2,1)S(1)} collective-permute-done((bf16[128,3072]{1,0:T(8,128)(2,1)S(1)}, bf16[128,3072]{1,0:T(8,128)(2,1)S(1)}, u32[]{:S(2)}, u32[]{:S(2)}) %collective-permute-start.16) | collective-permute-done | bytes 786464 | tf_op jit(solution)/shard_map/ppermute | solution.py:255
  225.0 1.6 constant_dynamic-update-slice_fusion.2
  226.6 2.2 collective-permute-done.34
  229.3 2.1 collective-permute-start.21
  231.4 2.2 collective-permute-start.19
  233.6 7.6 %fusion.9 = f32[768,3072]{1,0:T(8,128)} fusion(bf16[1024,768]{1,0:T(8,128)(2,1)S(1)} %bitcast.74, bf16[1024,3072]{1,0:T(8,128)(2,1)S(1)} %constant_dynamic-update-slice_fusion), kind=kOutput, calls=%fused_computation.30 | convolution fusion | flops 4831838208 | bytes 17301504 | tf_op jit(solution)/shard_map/dot_general | solution.py:332
  (65 shorter events, 10.6 us)
Async XLA Ops:
  2.7 13.4 %collective-permute-start.2 = (bf16[256,768]{1,0:T(8,128)(2,1)}, bf16[256,768]{1,0:T(8,128)(2,1)S(1)}, u32[]{:S(2)}, u32[]{:S(2)}) collective-permute-start(bf16[256,768]{1,0:T(8,128)(2,1)} %scale.1), channel_id=1, source_target_pairs={{0,32},{16,48},{32,64},{48,80},{64,96},{80,112},{96,0},{112,16},{1... | collective-permute-start | bytes 1179656 | tf_op jit(solution)/shard_map/ppermute | solution.py:255
  4.7 21.0 %collective-permute-start.1 = (bf16[256,768]{1,0:T(8,128)(2,1)}, bf16[256,768]{1,0:T(8,128)(2,1)S(1)}, u32[]{:S(2)}, u32[]{:S(2)}) collective-permute-start(bf16[256,768]{1,0:T(8,128)(2,1)} %scale.1), channel_id=1, source_target_pairs={{0,64},{16,80},{32,96},{48,112},{64,0},{80,16},{96,32},{112,48},{1... | collective-permute-start | bytes 1179656 | tf_op jit(solution)/shard_map/ppermute | solution.py:255
  8.3 17.5 %collective-permute-start = (bf16[256,768]{1,0:T(8,128)(2,1)}, bf16[256,768]{1,0:T(8,128)(2,1)S(1)}, u32[]{:S(2)}, u32[]{:S(2)}) collective-permute-start(bf16[256,768]{1,0:T(8,128)(2,1)} %scale.1), channel_id=1, source_target_pairs={{0,96},{16,112},{32,0},{48,16},{64,32},{80,48},{96,64},{112,80},{1... | collective-permute-start | bytes 1179656 | tf_op jit(solution)/shard_map/ppermute | solution.py:255
  26.8 3.5 %collective-permute-start.3 = (bf16[1024,768]{1,0:T(8,128)(2,1)S(1)}, bf16[1024,768]{1,0:T(8,128)(2,1)S(1)}, u32[]{:S(2)}, u32[]{:S(2)}) collective-permute-start(bf16[1024,768]{1,0:T(8,128)(2,1)S(1)} %pad_maximum_fusion.1), channel_id=1, source_target_pairs={{0,16},{16,0},{32,48},{48,32},{64,80},{80,64},{96,112},{112,96},{1... | collective-permute-start | bytes 4718600 | tf_op jit(solution)/shard_map/ppermute | solution.py:255
  35.6 28.6 %collective-permute-start.4 = (bf16[256,1536]{1,0:T(8,128)(2,1)S(1)}, bf16[256,1536]{1,0:T(8,128)(2,1)S(1)}, u32[]{:S(2)}, u32[]{:S(2)}) collective-permute-start(bf16[256,1536]{1,0:T(8,128)(2,1)S(1)} %get-tuple-element.63), channel_id=1, source_target_pairs={{0,4},{1,5},{2,6},{3,7},{4,8},{5,9},{6,10},{7,11},{8,12},{9,13},{1... | collective-permute-start | bytes 2359304 | tf_op jit(solution)/shard_map/ppermute | solution.py:255
  37.2 27.0 %collective-permute-start.5 = (bf16[256,1536]{1,0:T(8,128)(2,1)S(1)}, bf16[256,1536]{1,0:T(8,128)(2,1)S(1)}, u32[]{:S(2)}, u32[]{:S(2)}) collective-permute-start(bf16[256,1536]{1,0:T(8,128)(2,1)S(1)} %get-tuple-element.64), channel_id=1, source_target_pairs={{0,12},{1,13},{2,14},{3,15},{4,0},{5,1},{6,2},{7,3},{8,4},{9,5},{1... | collective-permute-start | bytes 2359304 | tf_op jit(solution)/shard_map/ppermute | solution.py:255
  45.5 27.6 %collective-permute-start.22 = (bf16[256,1536]{1,0:T(8,128)(2,1)}, bf16[256,1536]{1,0:T(8,128)(2,1)}, u32[]{:S(2)}, u32[]{:S(2)}) collective-permute-start(bf16[256,1536]{1,0:T(8,128)(2,1)} %get-tuple-element.87), channel_id=1, source_target_pairs={{0,1},{1,2},{2,3},{3,0},{4,5},{5,6},{6,7},{7,4},{8,9},{9,10},{10,1... | collective-permute-start | bytes 2359304 | tf_op jit(solution)/shard_map/ppermute | solution.py:255
  47.1 26.0 %collective-permute-start.23 = (bf16[256,1536]{1,0:T(8,128)(2,1)}, bf16[256,1536]{1,0:T(8,128)(2,1)}, u32[]{:S(2)}, u32[]{:S(2)}) collective-permute-start(bf16[256,1536]{1,0:T(8,128)(2,1)} %get-tuple-element.88), channel_id=1, source_target_pairs={{0,3},{1,0},{2,1},{3,2},{4,7},{5,4},{6,5},{7,6},{8,11},{9,8},{10,9... | collective-permute-start | bytes 2359304 | tf_op jit(solution)/shard_map/ppermute | solution.py:255
  64.2 0.9 copy-start.2
  65.1 1.0 copy-start.3
  69.9 10.3 %copy-start.6 = (s32[4]{0:T(128)S(1)}, s32[4]{0:T(128)}, u32[]{:S(2)}) copy-start(s32[4]{0:T(128)} %constant.60.clone) | copy-start | bytes 52
  69.9 36.9 %collective-permute-start.6 = (bf16[256,3072]{1,0:T(8,128)(2,1)}, bf16[256,3072]{1,0:T(8,128)(2,1)}, u32[]{:S(2)}, u32[]{:S(2)}) collective-permute-start(bf16[256,3072]{1,0:T(8,128)(2,1)} %get-tuple-element.65), channel_id=1, source_target_pairs={{0,4},{1,5},{2,6},{3,7},{4,8},{5,9},{6,10},{7,11},{8,12},{9,13},{1... | collective-permute-start | bytes 4718600 | tf_op jit(solution)/shard_map/ppermute | solution.py:255
  70.1 36.6 %collective-permute-start.7 = (bf16[256,3072]{1,0:T(8,128)(2,1)}, bf16[256,3072]{1,0:T(8,128)(2,1)}, u32[]{:S(2)}, u32[]{:S(2)}) collective-permute-start(bf16[256,3072]{1,0:T(8,128)(2,1)} %get-tuple-element.66), channel_id=1, source_target_pairs={{0,12},{1,13},{2,14},{3,15},{4,0},{5,1},{6,2},{7,3},{8,4},{9,5},{1... | collective-permute-start | bytes 4718600 | tf_op jit(solution)/shard_map/ppermute | solution.py:255
  76.9 40.5 %collective-permute-start.24 = (bf16[256,3072]{1,0:T(8,128)(2,1)}, bf16[256,3072]{1,0:T(8,128)(2,1)}, u32[]{:S(2)}, u32[]{:S(2)}) collective-permute-start(bf16[256,3072]{1,0:T(8,128)(2,1)} %get-tuple-element.89), channel_id=1, source_target_pairs={{0,1},{1,2},{2,3},{3,0},{4,5},{5,6},{6,7},{7,4},{8,9},{9,10},{10,1... | collective-permute-start | bytes 4718600 | tf_op jit(solution)/shard_map/ppermute | solution.py:255
  77.3 40.1 %collective-permute-start.25 = (bf16[256,3072]{1,0:T(8,128)(2,1)}, bf16[256,3072]{1,0:T(8,128)(2,1)}, u32[]{:S(2)}, u32[]{:S(2)}) collective-permute-start(bf16[256,3072]{1,0:T(8,128)(2,1)} %get-tuple-element.90), channel_id=1, source_target_pairs={{0,3},{1,0},{2,1},{3,2},{4,7},{5,4},{6,5},{7,6},{8,11},{9,8},{10,9... | collective-permute-start | bytes 4718600 | tf_op jit(solution)/shard_map/ppermute | solution.py:255
  112.2 14.5 %collective-permute-start.8 = (bf16[64,3072]{1,0:T(8,128)(2,1)}, bf16[64,3072]{1,0:T(8,128)(2,1)}, u32[]{:S(2)}, u32[]{:S(2)}) collective-permute-start(bf16[64,3072]{1,0:T(8,128)(2,1)} %get-tuple-element.71), channel_id=1, source_target_pairs={{0,2},{1,3},{2,0},{3,1},{4,6},{5,7},{6,4},{7,5},{8,10},{9,11},{10,... | collective-permute-start | bytes 1179656 | tf_op jit(solution)/shard_map/ppermute | solution.py:255
  114.1 17.5 %collective-permute-start.9 = (bf16[64,3072]{1,0:T(8,128)(2,1)}, bf16[64,3072]{1,0:T(8,128)(2,1)}, u32[]{:S(2)}, u32[]{:S(2)}) collective-permute-start(bf16[64,3072]{1,0:T(8,128)(2,1)} %get-tuple-element.72), channel_id=1, source_target_pairs={{0,1},{1,2},{2,3},{3,0},{4,5},{5,6},{6,7},{7,4},{8,9},{9,10},{10,1... | collective-permute-start | bytes 1179656 | tf_op jit(solution)/shard_map/ppermute | solution.py:255
  114.8 16.8 %collective-permute-start.10 = (bf16[64,3072]{1,0:T(8,128)(2,1)}, bf16[64,3072]{1,0:T(8,128)(2,1)}, u32[]{:S(2)}, u32[]{:S(2)}) collective-permute-start(bf16[64,3072]{1,0:T(8,128)(2,1)} %get-tuple-element.73), channel_id=1, source_target_pairs={{0,3},{1,0},{2,1},{3,2},{4,7},{5,4},{6,5},{7,6},{8,11},{9,8},{10,9... | collective-permute-start | bytes 1179656 | tf_op jit(solution)/shard_map/ppermute | solution.py:255
  122.9 14.7 %collective-permute-start.26 = (bf16[64,3072]{1,0:T(8,128)(2,1)}, bf16[64,3072]{1,0:T(8,128)(2,1)S(1)}, u32[]{:S(2)}, u32[]{:S(2)}) collective-permute-start(bf16[64,3072]{1,0:T(8,128)(2,1)} %get-tuple-element.95), channel_id=1, source_target_pairs={{0,8},{1,9},{2,10},{3,11},{4,12},{5,13},{6,14},{7,15},{8,0},{9,1},... | collective-permute-start | bytes 1179656 | tf_op jit(solution)/shard_map/ppermute | solution.py:255
  124.4 17.0 %collective-permute-start.27 = (bf16[64,3072]{1,0:T(8,128)(2,1)}, bf16[64,3072]{1,0:T(8,128)(2,1)}, u32[]{:S(2)}, u32[]{:S(2)}) collective-permute-start(bf16[64,3072]{1,0:T(8,128)(2,1)} %get-tuple-element.96), channel_id=1, source_target_pairs={{0,4},{1,5},{2,6},{3,7},{4,8},{5,9},{6,10},{7,11},{8,12},{9,13},{1... | collective-permute-start | bytes 1179656 | tf_op jit(solution)/shard_map/ppermute | solution.py:255
  126.7 14.7 %collective-permute-start.28 = (bf16[64,3072]{1,0:T(8,128)(2,1)}, bf16[64,3072]{1,0:T(8,128)(2,1)}, u32[]{:S(2)}, u32[]{:S(2)}) collective-permute-start(bf16[64,3072]{1,0:T(8,128)(2,1)} %get-tuple-element.97), channel_id=1, source_target_pairs={{0,12},{1,13},{2,14},{3,15},{4,0},{5,1},{6,2},{7,3},{8,4},{9,5},{1... | collective-permute-start | bytes 1179656 | tf_op jit(solution)/shard_map/ppermute | solution.py:255
  135.0 13.8 %collective-permute-start.11 = (bf16[64,3072]{1,0:T(8,128)(2,1)}, bf16[64,3072]{1,0:T(8,128)(2,1)}, u32[]{:S(2)}, u32[]{:S(2)}) collective-permute-start(bf16[64,3072]{1,0:T(8,128)(2,1)} %get-tuple-element.77.mine_ref), channel_id=1, source_target_pairs={{0,2},{1,3},{2,0},{3,1},{4,6},{5,7},{6,4},{7,5},{8,10},{9,11},{10,... | collective-permute-start | bytes 1179656 | tf_op jit(solution)/shard_map/ppermute | solution.py:255
  136.8 19.5 %collective-permute-start.12 = (bf16[64,3072]{1,0:T(8,128)(2,1)}, bf16[64,3072]{1,0:T(8,128)(2,1)}, u32[]{:S(2)}, u32[]{:S(2)}) collective-permute-start(bf16[64,3072]{1,0:T(8,128)(2,1)} %get-tuple-element.77.mine_ref), channel_id=1, source_target_pairs={{0,1},{1,2},{2,3},{3,0},{4,5},{5,6},{6,7},{7,4},{8,9},{9,10},{10,1... | collective-permute-start | bytes 1179656 | tf_op jit(solution)/shard_map/ppermute | solution.py:255
  137.6 3.9 %copy-start.4 = (bf16[64,3072]{1,0:T(8,128)(2,1)}, bf16[64,3072]{1,0:T(8,128)(2,1)S(1)}, u32[]{:S(2)}) copy-start(bf16[64,3072]{1,0:T(8,128)(2,1)S(1)} %collective-permute-done.26.b_ref) | copy-start | bytes 1179652
  137.6 18.8 %collective-permute-start.13 = (bf16[64,3072]{1,0:T(8,128)(2,1)}, bf16[64,3072]{1,0:T(8,128)(2,1)}, u32[]{:S(2)}, u32[]{:S(2)}) collective-permute-start(bf16[64,3072]{1,0:T(8,128)(2,1)} %get-tuple-element.77.mine_ref), channel_id=1, source_target_pairs={{0,3},{1,0},{2,1},{3,2},{4,7},{5,4},{6,5},{7,6},{8,11},{9,8},{10,9... | collective-permute-start | bytes 1179656 | tf_op jit(solution)/shard_map/ppermute | solution.py:255
  145.1 17.9 %collective-permute-start.29 = (bf16[64,3072]{1,0:T(8,128)(2,1)}, bf16[64,3072]{1,0:T(8,128)(2,1)S(1)}, u32[]{:S(2)}, u32[]{:S(2)}) collective-permute-start(bf16[64,3072]{1,0:T(8,128)(2,1)} %slope.1.mine_ref), channel_id=1, source_target_pairs={{0,8},{1,9},{2,10},{3,11},{4,12},{5,13},{6,14},{7,15},{8,0},{9,1},... | collective-permute-start | bytes 1179656 | tf_op jit(solution)/shard_map/ppermute | solution.py:255
  146.3 20.1 %collective-permute-start.30 = (bf16[64,3072]{1,0:T(8,128)(2,1)}, bf16[64,3072]{1,0:T(8,128)(2,1)}, u32[]{:S(2)}, u32[]{:S(2)}) collective-permute-start(bf16[64,3072]{1,0:T(8,128)(2,1)} %slope.1.mine_ref), channel_id=1, source_target_pairs={{0,4},{1,5},{2,6},{3,7},{4,8},{5,9},{6,10},{7,11},{8,12},{9,13},{1... | collective-permute-start | bytes 1179656 | tf_op jit(solution)/shard_map/ppermute | solution.py:255
  148.9 18.5 %collective-permute-start.31 = (bf16[64,3072]{1,0:T(8,128)(2,1)}, bf16[64,3072]{1,0:T(8,128)(2,1)}, u32[]{:S(2)}, u32[]{:S(2)}) collective-permute-start(bf16[64,3072]{1,0:T(8,128)(2,1)} %slope.1.mine_ref), channel_id=1, source_target_pairs={{0,12},{1,13},{2,14},{3,15},{4,0},{5,1},{6,2},{7,3},{8,4},{9,5},{1... | collective-permute-start | bytes 1179656 | tf_op jit(solution)/shard_map/ppermute | solution.py:255
  159.8 40.3 %collective-permute-start.14 = (bf16[256,3072]{1,0:T(8,128)(2,1)}, bf16[256,3072]{1,0:T(8,128)(2,1)}, u32[]{:S(2)}, u32[]{:S(2)}) collective-permute-start(bf16[256,3072]{1,0:T(8,128)(2,1)} %in_order.2), channel_id=1, source_target_pairs={{0,4},{1,5},{2,6},{3,7},{4,8},{5,9},{6,10},{7,11},{8,12},{9,13},{1... | collective-permute-start | bytes 4718600 | tf_op jit(solution)/shard_map/ppermute | solution.py:255
  159.8 41.4 %collective-permute-start.15 = (bf16[256,3072]{1,0:T(8,128)(2,1)}, bf16[256,3072]{1,0:T(8,128)(2,1)}, u32[]{:S(2)}, u32[]{:S(2)}) collective-permute-start(bf16[256,3072]{1,0:T(8,128)(2,1)} %in_order.2), channel_id=1, source_target_pairs={{0,12},{1,13},{2,14},{3,15},{4,0},{5,1},{6,2},{7,3},{8,4},{9,5},{1... | collective-permute-start | bytes 4718600 | tf_op jit(solution)/shard_map/ppermute | solution.py:255
  163.0 4.4 %copy-start.5 = (bf16[64,3072]{1,0:T(8,128)(2,1)}, bf16[64,3072]{1,0:T(8,128)(2,1)S(1)}, u32[]{:S(2)}) copy-start(bf16[64,3072]{1,0:T(8,128)(2,1)S(1)} %collective-permute-done.29.far_ref) | copy-start | bytes 1179652
  170.9 36.8 %collective-permute-start.32 = (bf16[256,3072]{1,0:T(8,128)(2,1)}, bf16[256,3072]{1,0:T(8,128)(2,1)}, u32[]{:S(2)}, u32[]{:S(2)}) collective-permute-start(bf16[256,3072]{1,0:T(8,128)(2,1)} %in_order.3), channel_id=1, source_target_pairs={{0,1},{1,2},{2,3},{3,0},{4,5},{5,6},{6,7},{7,4},{8,9},{9,10},{10,1... | collective-permute-start | bytes 4718600 | tf_op jit(solution)/shard_map/ppermute | solution.py:255
  170.9 37.9 %collective-permute-start.33 = (bf16[256,3072]{1,0:T(8,128)(2,1)}, bf16[256,3072]{1,0:T(8,128)(2,1)}, u32[]{:S(2)}, u32[]{:S(2)}) collective-permute-start(bf16[256,3072]{1,0:T(8,128)(2,1)} %in_order.3), channel_id=1, source_target_pairs={{0,3},{1,0},{2,1},{3,2},{4,7},{5,4},{6,5},{7,6},{8,11},{9,8},{10,9... | collective-permute-start | bytes 4718600 | tf_op jit(solution)/shard_map/ppermute | solution.py:255
  174.3 2.7 %slice-start = ((s8[4718592]{0:T(1024)(128)(4,1)}), s8[4194304]{0:T(1024)(128)(4,1)S(1)}, s32[]{:S(2)}) async-start(s8[4718592]{0:T(1024)(128)(4,1)} %bitcast.70), calls=%async_computation | async-start | bytes 8388608
  174.5 1.6 copy-start
  174.5 2.6 %slice-start.1 = ((s8[4718592]{0:T(1024)(128)(4,1)}), s8[524288]{0:T(1024)(128)(4,1)S(1)}, s32[]{:S(2)}) async-start(s8[4718592]{0:T(1024)(128)(4,1)} %bitcast.70), calls=%async_computation.1 | async-start | bytes 1048576
  176.0 1.8 copy-start.1
  202.4 20.7 %collective-permute-start.16 = (bf16[128,3072]{1,0:T(8,128)(2,1)S(1)}, bf16[128,3072]{1,0:T(8,128)(2,1)S(1)}, u32[]{:S(2)}, u32[]{:S(2)}) collective-permute-start(bf16[128,3072]{1,0:T(8,128)(2,1)S(1)} %slice.45), channel_id=1, source_target_pairs={{0,4},{1,5},{2,6},{3,7},{4,8},{5,9},{6,10},{7,11},{8,12},{9,13},{1... | collective-permute-start | bytes 2359304 | tf_op jit(solution)/shard_map/ppermute | solution.py:255
  202.5 21.5 %collective-permute-start.17 = (bf16[128,3072]{1,0:T(8,128)(2,1)S(1)}, bf16[128,3072]{1,0:T(8,128)(2,1)S(1)}, u32[]{:S(2)}, u32[]{:S(2)}) collective-permute-start(bf16[128,3072]{1,0:T(8,128)(2,1)S(1)} %slice.46), channel_id=1, source_target_pairs={{0,12},{1,13},{2,14},{3,15},{4,0},{5,1},{6,2},{7,3},{8,4},{9,5},{1... | collective-permute-start | bytes 2359304 | tf_op jit(solution)/shard_map/ppermute | solution.py:255
  210.1 18.7 %collective-permute-start.34 = (bf16[128,3072]{1,0:T(8,128)(2,1)S(1)}, bf16[128,3072]{1,0:T(8,128)(2,1)S(1)}, u32[]{:S(2)}, u32[]{:S(2)}) collective-permute-start(bf16[128,3072]{1,0:T(8,128)(2,1)S(1)} %slice.53), channel_id=1, source_target_pairs={{0,1},{1,2},{2,3},{3,0},{4,5},{5,6},{6,7},{7,4},{8,9},{9,10},{10,1... | collective-permute-start | bytes 2359304 | tf_op jit(solution)/shard_map/ppermute | solution.py:255
  210.2 18.7 %collective-permute-start.35 = (bf16[128,3072]{1,0:T(8,128)(2,1)S(1)}, bf16[128,3072]{1,0:T(8,128)(2,1)S(1)}, u32[]{:S(2)}, u32[]{:S(2)}) collective-permute-start(bf16[128,3072]{1,0:T(8,128)(2,1)S(1)} %slice.54), channel_id=1, source_target_pairs={{0,3},{1,0},{2,1},{3,2},{4,7},{5,4},{6,5},{7,6},{8,11},{9,8},{10,9... | collective-permute-start | bytes 2359304 | tf_op jit(solution)/shard_map/ppermute | solution.py:255
  224.9 4.0 %collective-permute-start.18 = (bf16[512,768]{1,0:T(8,128)(2,1)S(1)}, bf16[512,768]{1,0:T(8,128)(2,1)S(1)}, u32[]{:S(2)}, u32[]{:S(2)}) collective-permute-start(bf16[512,768]{1,0:T(8,128)(2,1)S(1)} %bitcast.76), channel_id=1, source_target_pairs={{0,16},{16,0},{32,48},{48,32},{64,80},{80,64},{96,112},{112,96},{1... | collective-permute-start | bytes 2359304 | tf_op jit(solution)/shard_map/ppermute | solution.py:255
  229.3 11.9 %collective-permute-start.21 = (bf16[128,768]{1,0:T(8,128)(2,1)S(1)}, bf16[128,768]{1,0:T(8,128)(2,1)S(1)}, u32[]{:S(2)}, u32[]{:S(2)}) collective-permute-start(bf16[128,768]{1,0:T(8,128)(2,1)S(1)} %get-tuple-element.84), channel_id=1, source_target_pairs={{0,96},{16,112},{32,0},{48,16},{64,32},{80,48},{96,64},{112,80},{1... | collective-permute-start | bytes 589832 | tf_op jit(solution)/shard_map/ppermute | solution.py:255
  231.4 10.4 %collective-permute-start.20 = (bf16[128,768]{1,0:T(8,128)(2,1)S(1)}, bf16[128,768]{1,0:T(8,128)(2,1)S(1)}, u32[]{:S(2)}, u32[]{:S(2)}) collective-permute-start(bf16[128,768]{1,0:T(8,128)(2,1)S(1)} %get-tuple-element.83), channel_id=1, source_target_pairs={{0,32},{16,48},{32,64},{48,80},{64,96},{80,112},{96,0},{112,16},{1... | collective-permute-start | bytes 589832 | tf_op jit(solution)/shard_map/ppermute | solution.py:255
  231.4 10.4 %collective-permute-start.19 = (bf16[128,768]{1,0:T(8,128)(2,1)S(1)}, bf16[128,768]{1,0:T(8,128)(2,1)S(1)}, u32[]{:S(2)}, u32[]{:S(2)}) collective-permute-start(bf16[128,768]{1,0:T(8,128)(2,1)S(1)} %get-tuple-element.82), channel_id=1, source_target_pairs={{0,64},{16,80},{32,96},{48,112},{64,0},{80,16},{96,32},{112,48},{1... | collective-permute-start | bytes 589832 | tf_op jit(solution)/shard_map/ppermute | solution.py:255
where the time goes:
time: 244 us; the launch traced here: 243 us
  waiting for transfers between devices  87.3 us (36%)
  Pallas kernels  61.9 us (25%)
  starting transfers between devices  59.7 us (24%)
  matrix products  16.4 us (7%)
  local copies, waits for them, and re-layouts  13.6 us (6%)
  other arithmetic  2.82 us (1%)
    ppermute x36, waiting for transfers between devices, send(): lax.ppermute(a, 'col' if axis in ('x', 'y') else 'row', steps_on(axis, st...  87.3 us
    ppermute x36, starting transfers between devices, send(): lax.ppermute(a, 'col' if axis in ('x', 'y') else 'row', steps_on(axis, st...  59.7 us
    pallas_call x4, Pallas kernels, call(): pl.pallas_call(functools.partial(kernel, self.tensor), grid_spec=grid, ou...  27.3 us
    pallas_call x2, Pallas kernels, row_blocks(): pl.pallas_call(blocks_kernel, grid_spec=grid, out_shape=[pltpu.HBM((small...  11 us
    dot_general x5, matrix products, local(): term = jnp.dot(block, down_weight, preferred_element_type=F32)  8.79 us
    dot_general x1, matrix products, local(): lax.dot_general(crossed, whole, (((0,), (0,)), ((), ())), preferred_eleme...  7.59 us
    pallas_call x2, Pallas kernels, add(): pl.pallas_call(add_kernel, grid_spec=grid, out_shape=[pltpu.HBM(after.sha...  7.55 us
    pallas_call x2, Pallas kernels, by_tiles(): pl.pallas_call(kernel, grid=(3,), in_specs=[spec] * len(ins), out_specs=[...  7.08 us
  transfers between devices with their start and end apart: 36, of which 15 were waited for; matrix products, arithmetic and copies ran while one was open for 11% of the time, Pallas kernels for 22%

commit v1 on v0

--- a/solution.py
+++ b/solution.py
@@ -10,6 +10,7 @@
 BLOCK = 128
 SIDE = 4
 TILES = 6
+PIECES = 3
 BF16 = jnp.bfloat16
 F32 = jnp.float32
 COST = pl.CostEstimate(flops=1000, bytes_accessed=1000, transcendentals=0)
@@ -43,23 +44,28 @@
     )(x_values, x_scales, grad_values, grad_scales)
 
 
-def share_dot(tensor, take, same_ref, other_ref, w_ref):
+def share_dot(tensor, take, same_ref, other_ref, w_refs):
     width = same_ref.shape[-1]
     if tensor == 0:
         a = jnp.concatenate([r[...].reshape(-1, width) for r in (same_ref, other_ref)], axis=0)
     else:
         a = jnp.where(take == 0, same_ref[...], other_ref[...]).reshape(-1, width)
     dims = (((1,), (tensor,)), ((), ()))
-    return lax.dot_general(a, w_ref[...], dims, preferred_element_type=F32)
+    n = width // len(w_refs)
+    return sum(
+        lax.dot_general(a[:, k * n : (k + 1) * n], w[...], dims, preferred_element_type=F32)
+        for k, w in enumerate(w_refs)
+    )
 
 
 def core_of(slot_ref, step):
     return lax.div(lax.rem(slot_ref[0] + step, SIDE), 2)
 
 
-def far_kernel(tensor, slot_ref, same_ref, other_ref, w_ref, low_ref, high_ref):
+def far_kernel(tensor, slot_ref, same_ref, other_ref, *refs):
+    w_refs, (low_ref, high_ref) = refs[:PIECES], refs[PIECES:]
     j, half = pl.program_id(0), pl.num_programs(0) // 2
-    out = share_dot(tensor, core_of(slot_ref, 2), same_ref, other_ref, w_ref).astype(BF16)
+    out = share_dot(tensor, core_of(slot_ref, 2), same_ref, other_ref, w_refs).astype(BF16)
 
     @pl.when(j < half)
     def _():
@@ -71,10 +77,10 @@
 
 
 def near_kernel(tensor, slot_ref, *refs):
-    w_ref, outs = refs[6], refs[7:]
+    w_refs, outs = refs[6 : 6 + PIECES], refs[6 + PIECES :]
     for i, step in enumerate((1, 3, 0)):
         same_ref, other_ref = refs[2 * i : 2 * i + 2]
-        out = share_dot(tensor, core_of(slot_ref, step), same_ref, other_ref, w_ref)
+        out = share_dot(tensor, core_of(slot_ref, step), same_ref, other_ref, w_refs)
         outs[i][...] = out.astype(BF16)
 
 
@@ -83,32 +89,32 @@
     before_out[...] = (before_ref[...].astype(F32) + high_ref[...].astype(F32)).astype(BF16)
 
 
-def blocks_kernel(slots_ref, a_ref, b_ref, c_ref, *outs):
-    total = sum(r[...].astype(F32) for r in (a_ref, b_ref, c_ref))
+def blocks_kernel(slot_ref, *refs):
+    ins, outs = refs[: 3 * SIDE], refs[3 * SIDE :]
     for i, out in enumerate(outs):
-
-        @pl.when(pl.program_id(0) == i)
-        def _():
-            out[...] = total.astype(out.dtype)
+        out[...] = sum(r[...].astype(F32) for r in ins[3 * i : 3 * i + 3]).astype(out.dtype)
 
 
 def row_blocks(terms, place):
     big, units = terms[0].shape
-    small = big // SIDE
-    slots = lax.rem(place + jnp.array([2, 1, 3, 0], jnp.int32), SIDE)
+    shape = (big // SIDE, units // 2)
+    ins = [
+        pl.BlockSpec(shape, lambda j, slot, step=step: (lax.rem(slot[0] + step, SIDE), j))
+        for step in (2, 1, 3, 0)
+    ]
     grid = pltpu.PrefetchScalarGridSpec(
         num_scalar_prefetch=1,
-        grid=(SIDE,),
-        in_specs=[pl.BlockSpec((small, units), lambda j, slots: (slots[j], 0))] * 3,
-        out_specs=[pl.BlockSpec((small, units), lambda j, slots: (0, 0))] * 4,
+        grid=(2,),
+        in_specs=[spec for spec in ins for _ in range(3)],
+        out_specs=[pl.BlockSpec(shape, lambda j, slot: (0, j))] * 4,
     )
     return pl.pallas_call(
         blocks_kernel,
         grid_spec=grid,
-        out_shape=[pltpu.HBM((small, units), kind) for kind in (BF16, BF16, BF16, F32)],
+        out_shape=[pltpu.HBM((big // SIDE, units), kind) for kind in (BF16, BF16, BF16, F32)],
         cost_estimate=COST,
         name="row_blocks",
-    )(slots, *terms)
+    )(place.reshape(1), *(list(terms) * SIDE))
 
 
 def act_kernel(a_ref, b_ref, c_ref, d_ref, pre_ref, hidden_ref):
@@ -184,16 +190,19 @@
             return pl.BlockSpec((1, 1, 2, self.small, self.width), along_x)
         return pl.BlockSpec((SIDE, 1, 1, self.small, self.width), along_y)
 
-    def weight_spec(self):
+    def weight_specs(self):
+        n = self.width // PIECES
         if self.tensor == 0:
-            return pl.BlockSpec((self.width, self.tile), lambda j, slot: (0, j))
-        return pl.BlockSpec((self.tile, self.width), lambda j, slot: (j, 0))
+            return [
+                pl.BlockSpec((n, self.tile), lambda j, slot, k=k: (k, j)) for k in range(PIECES)
+            ]
+        return [pl.BlockSpec((self.tile, n), lambda j, slot, k=k: (j, k)) for k in range(PIECES)]
 
     def call(self, kernel, place, held, steps, outs, specs, name):
         grid = pltpu.PrefetchScalarGridSpec(
             num_scalar_prefetch=1,
             grid=(TILES,),
-            in_specs=[self.rows_spec(step) for step in steps for _ in held] + [self.weight_spec()],
+            in_specs=[self.rows_spec(step) for step in steps for _ in held] + self.weight_specs(),
             out_specs=specs,
         )
         return pl.pallas_call(
@@ -203,10 +212,10 @@
             compiler_params=pltpu.CompilerParams(vmem_limit_bytes=24 * 1024 * 1024),
             cost_estimate=COST,
             name=name,
-        )(place.reshape(1), *(held * len(steps)), in_hbm(self.weight))
+        )(place.reshape(1), *(held * len(steps)), *([in_hbm(self.weight)] * PIECES))
 
     def far(self, place, held):
-        half = jax.ShapeDtypeStruct((self.big, self.units // 2), BF16)
+        half = pltpu.HBM((self.big, self.units // 2), BF16)
         last = TILES // 2 - 1
         shape = (self.big, self.tile)
         specs = [

time: 244 us -> 240 us (0.984)
  starting transfers between devices: 59.7 us -> 56.7 us
  Pallas kernels: 61.9 us -> 59.2 us
  waiting for transfers between devices: 87.3 us -> 89.8 us
    pallas_call x2, Pallas kernels: 11 us -> 7.42 us  [row_blocks(): pl.pallas_call(blocks_kernel, grid_spec=grid, out_shape=[pltpu.HBM((big /...]
    ppermute x36, starting transfers between devices: 59.7 us -> 56.7 us  [send(): lax.ppermute(a, 'col' if axis in ('x', 'y') else 'row', steps_on(axis, st...]
    ppermute x36, waiting for transfers between devices: 87.3 us -> 89.8 us  [send(): lax.ppermute(a, 'col' if axis in ('x', 'y') else 'row', steps_on(axis, st...]
  transfers between devices with their start and end apart: 36 -> 36, of which waited for: 15 -> 14; matrix products, arithmetic and copies ran while one was open for 11% -> 11% of each run, Pallas kernels for 22% -> 21%
where the time goes in v1:
time: 240 us; the launch traced here: 237 us
  waiting for transfers between devices  89.8 us (37%)
  Pallas kernels  59.2 us (25%)
  starting transfers between devices  56.7 us (24%)
  matrix products  16.4 us (7%)
  local copies, waits for them, and re-layouts  11.7 us (5%)
    ppermute x36, waiting for transfers between devices, send(): lax.ppermute(a, 'col' if axis in ('x', 'y') else 'row', steps_on(axis, st...  89.8 us
    ppermute x36, starting transfers between devices, send(): lax.ppermute(a, 'col' if axis in ('x', 'y') else 'row', steps_on(axis, st...  56.7 us
    pallas_call x4, Pallas kernels, call(): pl.pallas_call(functools.partial(kernel, self.tensor), grid_spec=grid, ou...  28.1 us
    dot_general x5, matrix products, local(): term = jnp.dot(block, down_weight, preferred_element_type=F32)  8.8 us
    pallas_call x2, Pallas kernels, add(): pl.pallas_call(add_kernel, grid_spec=grid, out_shape=[pltpu.HBM(after.sha...  7.65 us
    dot_general x1, matrix products, local(): lax.dot_general(crossed, whole, (((0,), (0,)), ((), ())), preferred_eleme...  7.59 us
    pallas_call x2, Pallas kernels, row_blocks(): pl.pallas_call(blocks_kernel, grid_spec=grid, out_shape=[pltpu.HBM((big /...  7.42 us
    pallas_call x2, Pallas kernels, by_tiles(): pl.pallas_call(kernel, grid=(3,), in_specs=[spec] * len(ins), out_specs=[...  7.09 us
  transfers between devices with their start and end apart: 36, of which 14 were waited for; matrix products, arithmetic and copies ran while one was open for 11% of the time, Pallas kernels for 21%

profile of v1, /device:TPU:0, one launch (start us, length us, event | category | flops | bytes accessed | tf_op | source)
XLA Modules:
  0.0 237.0 jit_solution(11248937004243236397)
XLA Ops:
  0.6 2.0 scale.1
  2.7 2.0 collective-permute-start.2
  4.7 3.6 %collective-permute-start.1 = (bf16[256,768]{1,0:T(8,128)(2,1)}, bf16[256,768]{1,0:T(8,128)(2,1)S(1)}, u32[]{:S(2)}, u32[]{:S(2)}) collective-permute-start(bf16[256,768]{1,0:T(8,128)(2,1)} %scale.1), channel_id=1, source_target_pairs={{0,64},{16,80},{32,96},{48,112},{64,0},{80,16},{96,32},{112,48},{1... | collective-permute-start | bytes 1179656 | tf_op jit(solution)/shard_map/ppermute | solution.py:264
  8.3 1.0 collective-permute-start
  9.3 6.9 %collective-permute-done.2 = bf16[256,768]{1,0:T(8,128)(2,1)S(1)} collective-permute-done((bf16[256,768]{1,0:T(8,128)(2,1)}, bf16[256,768]{1,0:T(8,128)(2,1)S(1)}, u32[]{:S(2)}, u32[]{:S(2)}) %collective-permute-start.2) | collective-permute-done | bytes 393248 | tf_op jit(solution)/shard_map/ppermute | solution.py:264
  16.1 9.6 %collective-permute-done.1 = bf16[256,768]{1,0:T(8,128)(2,1)S(1)} collective-permute-done((bf16[256,768]{1,0:T(8,128)(2,1)}, bf16[256,768]{1,0:T(8,128)(2,1)S(1)}, u32[]{:S(2)}, u32[]{:S(2)}) %collective-permute-start.1) | collective-permute-done | bytes 393248 | tf_op jit(solution)/shard_map/ppermute | solution.py:264
  25.7 1.1 pad_maximum_fusion.1
  26.9 3.4 %collective-permute-done.3 = bf16[1024,768]{1,0:T(8,128)(2,1)S(1)} collective-permute-done((bf16[1024,768]{1,0:T(8,128)(2,1)S(1)}, bf16[1024,768]{1,0:T(8,128)(2,1)S(1)}, u32[]{:S(2)}, u32[]{:S(2)}) %collective-permute-start.3) | collective-permute-done | bytes 1572896 | tf_op jit(solution)/shard_map/ppermute | solution.py:264
  30.3 6.4 %far_share.2 = (bf16[256,1536]{1,0:T(8,128)(2,1)}, bf16[256,1536]{1,0:T(8,128)(2,1)}) custom-call(s32[1]{0:T(128)} %bitcast.6.slot_ref, bf16[4,2,2,64,768]{4,3,2,1,0:T(8,128)(2,1)S(1)} %bitcast.52, bf16[4,2,2,64,768]{4,3,2,1,0:T(8,128)(2,1)S(1)} %bitcast.61, bf16[768,3072]{1,0:T(8,128)(2,1)} %refs_2_.2, bf16[768,3072]{1,0:T(8,128)(2,1)} %refs_2_.2, ...), custom_call_target="tpu_custom_call" | custom-call | flops 1000 | bytes 1000 | tf_op jit(solution)/shard_map/far_share/pallas_call | solution.py:208
  36.7 1.5 collective-permute-start.4
  38.2 1.7 collective-permute-start.5
  39.9 6.5 %far_share.3 = (bf16[256,1536]{1,0:T(8,128)(2,1)}, bf16[256,1536]{1,0:T(8,128)(2,1)}) custom-call(s32[1]{0:T(128)} %bitcast.20.slot_ref, bf16[4,2,2,64,768]{4,3,2,1,0:T(8,128)(2,1)S(1)} %bitcast.53, bf16[4,2,2,64,768]{4,3,2,1,0:T(8,128)(2,1)S(1)} %bitcast.62, bf16[3072,768]{1,0:T(8,128)(2,1)} %refs_2_.3, bf16[3072,768]{1,0:T(8,128)(2,1)} %refs_2_.3, ...), custom_call_target="tpu_custom_call" | custom-call | flops 1000 | bytes 1000 | tf_op jit(solution)/shard_map/far_share/pallas_call | solution.py:208
  46.4 1.6 collective-permute-start.22
  48.0 1.7 collective-permute-start.23
  49.6 7.5 %near_shares.2 = (bf16[256,3072]{1,0:T(8,128)(2,1)}, bf16[256,3072]{1,0:T(8,128)(2,1)}, bf16[256,3072]{1,0:T(8,128)(2,1)}) custom-call(s32[1]{0:T(128)} %bitcast.1.slot_ref, bf16[4,2,2,64,768]{4,3,2,1,0:T(8,128)(2,1)S(1)} %bitcast.54, bf16[4,2,2,64,768]{4,3,2,1,0:T(8,128)(2,1)S(1)} %bitcast.63, bf16[4,2,2,64,768]{4,3,2,1,0:T(8,128)(2,1)S(1)} %bitcast.55, ...), custom_call_target="tpu_custom_call" | custom-call | flops 1000 | bytes 1000 | tf_op jit(solution)/shard_map/near_shares/pallas_call | solution.py:208
  57.2 7.8 %near_shares.3 = (bf16[256,3072]{1,0:T(8,128)(2,1)}, bf16[256,3072]{1,0:T(8,128)(2,1)}, bf16[256,3072]{1,0:T(8,128)(2,1)}) custom-call(s32[1]{0:T(128)} %bitcast.4.slot_ref, bf16[4,2,2,64,768]{4,3,2,1,0:T(8,128)(2,1)S(1)} %bitcast.57, bf16[4,2,2,64,768]{4,3,2,1,0:T(8,128)(2,1)S(1)} %bitcast.66, bf16[4,2,2,64,768]{4,3,2,1,0:T(8,128)(2,1)S(1)} %bitcast.58, ...), custom_call_target="tpu_custom_call" | custom-call | flops 1000 | bytes 1000 | tf_op jit(solution)/shard_map/near_shares/pallas_call | solution.py:208
  64.9 3.8 %add_far.2 = (bf16[256,3072]{1,0:T(8,128)(2,1)}, bf16[256,3072]{1,0:T(8,128)(2,1)}) custom-call(s32[1]{0:T(128)} %bitcast.5.slot_ref, bf16[256,3072]{1,0:T(8,128)(2,1)} %get-tuple-element.61.after_ref, bf16[256,3072]{1,0:T(8,128)(2,1)} %get-tuple-element.62.before_ref, ...), custom_call_target="tpu_custom_call", output_to_operand_aliasing={{0}: (1, {}), {1}: (2, {})} | custom-call | flops 1000 | bytes 1000 | tf_op jit(solution)/shard_map/add_far/pallas_call | solution.py:243
  69.0 2.9 %collective-permute-start.7 = (bf16[256,3072]{1,0:T(8,128)(2,1)}, bf16[256,3072]{1,0:T(8,128)(2,1)}, u32[]{:S(2)}, u32[]{:S(2)}) collective-permute-start(bf16[256,3072]{1,0:T(8,128)(2,1)} %get-tuple-element.66), channel_id=1, source_target_pairs={{0,12},{1,13},{2,14},{3,15},{4,0},{5,1},{6,2},{7,3},{8,4},{9,5},{1... | collective-permute-start | bytes 4718600 | tf_op jit(solution)/shard_map/ppermute | solution.py:264
  72.0 3.9 %add_far.3 = (bf16[256,3072]{1,0:T(8,128)(2,1)}, bf16[256,3072]{1,0:T(8,128)(2,1)}) custom-call(s32[1]{0:T(128)} %bitcast.20.slot_ref, bf16[256,3072]{1,0:T(8,128)(2,1)} %get-tuple-element.85.after_ref, bf16[256,3072]{1,0:T(8,128)(2,1)} %get-tuple-element.86.before_ref, ...), custom_call_target="tpu_custom_call", output_to_operand_aliasing={{0}: (1, {}), {1}: (2, {})} | custom-call | flops 1000 | bytes 1000 | tf_op jit(solution)/shard_map/add_far/pallas_call | solution.py:243
  76.2 2.9 %collective-permute-start.25 = (bf16[256,3072]{1,0:T(8,128)(2,1)}, bf16[256,3072]{1,0:T(8,128)(2,1)}, u32[]{:S(2)}, u32[]{:S(2)}) collective-permute-start(bf16[256,3072]{1,0:T(8,128)(2,1)} %get-tuple-element.90), channel_id=1, source_target_pairs={{0,3},{1,0},{2,1},{3,2},{4,7},{5,4},{6,5},{7,6},{8,11},{9,8},{10,9... | collective-permute-start | bytes 4718600 | tf_op jit(solution)/shard_map/ppermute | solution.py:264
  79.1 26.6 %collective-permute-done.6.refs_1_.refs_4_.refs_7_.refs_10_ = bf16[256,3072]{1,0:T(8,128)(2,1)} collective-permute-done((bf16[256,3072]{1,0:T(8,128)(2,1)}, bf16[256,3072]{1,0:T(8,128)(2,1)}, u32[]{:S(2)}, u32[]{:S(2)}) %collective-permute-start.6) | collective-permute-done | bytes 1572896 | tf_op jit(solution)/shard_map/ppermute | solution.py:264
  105.6 3.7 %row_blocks.2 = (bf16[64,3072]{1,0:T(8,128)(2,1)}, bf16[64,3072]{1,0:T(8,128)(2,1)}, bf16[64,3072]{1,0:T(8,128)(2,1)}, f32[64,3072]{1,0:T(8,128)}) custom-call(s32[1]{0:T(128)} %bitcast.slot_ref, bf16[256,3072]{1,0:T(8,128)(2,1)} %get-tuple-element.57.refs_0_.refs_3_.refs_6_.refs_9_, ...), custom_call_target="tpu_custom_call" | custom-call | flops 1000 | bytes 1000 | tf_op jit(solution)/shard_map/row_blocks/pallas_call | solution.py:111
  109.3 2.0 collective-permute-start.8
  112.0 2.6 %collective-permute-start.10 = (bf16[64,3072]{1,0:T(8,128)(2,1)}, bf16[64,3072]{1,0:T(8,128)(2,1)}, u32[]{:S(2)}, u32[]{:S(2)}) collective-permute-start(bf16[64,3072]{1,0:T(8,128)(2,1)} %get-tuple-element.73), channel_id=1, source_target_pairs={{0,3},{1,0},{2,1},{3,2},{4,7},{5,4},{6,5},{7,6},{8,11},{9,8},{10,9... | collective-permute-start | bytes 1179656 | tf_op jit(solution)/shard_map/ppermute | solution.py:264
  114.6 5.9 %collective-permute-done.25.refs_2_.refs_5_.refs_8_.refs_11_ = bf16[256,3072]{1,0:T(8,128)(2,1)} collective-permute-done((bf16[256,3072]{1,0:T(8,128)(2,1)}, bf16[256,3072]{1,0:T(8,128)(2,1)}, u32[]{:S(2)}, u32[]{:S(2)}) %collective-permute-start.25) | collective-permute-done | bytes 1572896 | tf_op jit(solution)/shard_map/ppermute | solution.py:264
  120.5 3.7 %row_blocks.3 = (bf16[64,3072]{1,0:T(8,128)(2,1)}, bf16[64,3072]{1,0:T(8,128)(2,1)}, bf16[64,3072]{1,0:T(8,128)(2,1)}, f32[64,3072]{1,0:T(8,128)}) custom-call(s32[1]{0:T(128)} %bitcast.6.slot_ref, bf16[256,3072]{1,0:T(8,128)(2,1)} %get-tuple-element.59.refs_0_.refs_3_.refs_6_.refs_9_, ...), custom_call_target="tpu_custom_call" | custom-call | flops 1000 | bytes 1000 | tf_op jit(solution)/shard_map/row_blocks/pallas_call | solution.py:111
  124.4 3.2 %collective-permute-start.28 = (bf16[64,3072]{1,0:T(8,128)(2,1)}, bf16[64,3072]{1,0:T(8,128)(2,1)}, u32[]{:S(2)}, u32[]{:S(2)}) collective-permute-start(bf16[64,3072]{1,0:T(8,128)(2,1)} %get-tuple-element.97), channel_id=1, source_target_pairs={{0,12},{1,13},{2,14},{3,15},{4,0},{5,1},{6,2},{7,3},{8,4},{9,5},{1... | collective-permute-start | bytes 1179656 | tf_op jit(solution)/shard_map/ppermute | solution.py:264
  127.6 1.4 collective-permute-done.9.c_ref
  129.0 3.4 %act.1 = (f32[64,3072]{1,0:T(8,128)}, bf16[64,3072]{1,0:T(8,128)(2,1)}) custom-call(f32[64,3072]{1,0:T(8,128)} %get-tuple-element.67.a_ref, bf16[64,3072]{1,0:T(8,128)(2,1)} %collective-permute-done.8.b_ref, bf16[64,3072]{1,0:T(8,128)(2,1)} %collective-permute-done.9.c_ref, bf16[64,3072]{1,0:T(8,128)(2,1)} %collective-permute-done.10.d_ref), custom_call_target="tpu_custom_call" | custom-call | flops 1000 | bytes 1000 | tf_op jit(solution)/shard_map/act/pallas_call | solution.py:134
  132.4 1.7 collective-permute-start.11
  134.2 2.1 collective-permute-start.12
  136.2 1.8 collective-permute-start.13
  138.1 3.7 %slope.1.mine_ref = bf16[64,3072]{1,0:T(8,128)(2,1)} custom-call(f32[64,3072]{1,0:T(8,128)} %get-tuple-element.91.a_ref, bf16[64,3072]{1,0:T(8,128)(2,1)} %copy-done.2, bf16[64,3072]{1,0:T(8,128)(2,1)} %collective-permute-done.27.c_ref, bf16[64,3072]{1,0:T(8,128)(2,1)} %collective-permute-done.28.d_ref, f32[64,3072]{1,0:T(8,128)} %get-tuple-element.98.pre_ref), custom_call_target="tpu_custom_call" | custom-call | flops 1000 | bytes 1000 | tf_op jit(solution)/shard_map/slope/pallas_call | solution.py:134
  141.8 0.9 collective-permute-start.29
  142.7 1.8 collective-permute-start.30
  144.5 1.8 collective-permute-done.11.far_ref
  146.3 2.5 %collective-permute-start.31 = (bf16[64,3072]{1,0:T(8,128)(2,1)}, bf16[64,3072]{1,0:T(8,128)(2,1)}, u32[]{:S(2)}, u32[]{:S(2)}) collective-permute-start(bf16[64,3072]{1,0:T(8,128)(2,1)} %slope.1.mine_ref), channel_id=1, source_target_pairs={{0,12},{1,13},{2,14},{3,15},{4,0},{5,1},{6,2},{7,3},{8,4},{9,5},{1... | collective-permute-start | bytes 1179656 | tf_op jit(solution)/shard_map/ppermute | solution.py:264
  148.7 5.0 %collective-permute-done.12.before_ref = bf16[64,3072]{1,0:T(8,128)(2,1)} collective-permute-done((bf16[64,3072]{1,0:T(8,128)(2,1)}, bf16[64,3072]{1,0:T(8,128)(2,1)}, u32[]{:S(2)}, u32[]{:S(2)}) %collective-permute-start.12) | collective-permute-done | bytes 393248 | tf_op jit(solution)/shard_map/ppermute | solution.py:264
  153.8 3.4 %in_order.2 = bf16[256,3072]{1,0:T(8,128)(2,1)} custom-call(s32[1]{0:T(128)} %bitcast.slot_ref, bf16[64,3072]{1,0:T(8,128)(2,1)} %get-tuple-element.77.mine_ref, bf16[64,3072]{1,0:T(8,128)(2,1)} %collective-permute-done.11.far_ref, bf16[64,3072]{1,0:T(8,128)(2,1)} %collective-permute-done.12.before_ref, bf16[64,3072]{1,0:T(8,128)(2,1)} %collective-permute-done.13.after_ref), custom_call_target="tpu_custom_call" | custom-call | flops 1000 | bytes 1000 | tf_op jit(solution)/shard_map/in_order/pallas_call | solution.py:161
  157.2 3.2 %collective-permute-start.15 = (bf16[256,3072]{1,0:T(8,128)(2,1)}, bf16[256,3072]{1,0:T(8,128)(2,1)}, u32[]{:S(2)}, u32[]{:S(2)}) collective-permute-start(bf16[256,3072]{1,0:T(8,128)(2,1)} %in_order.2), channel_id=1, source_target_pairs={{0,12},{1,13},{2,14},{3,15},{4,0},{5,1},{6,2},{7,3},{8,4},{9,5},{1... | collective-permute-start | bytes 4718600 | tf_op jit(solution)/shard_map/ppermute | solution.py:264
  160.4 0.8 collective-permute-done.30.before_ref
  161.3 1.2 collective-permute-done.31.after_ref
  162.5 3.5 %in_order.3 = bf16[256,3072]{1,0:T(8,128)(2,1)} custom-call(s32[1]{0:T(128)} %bitcast.6.slot_ref, bf16[64,3072]{1,0:T(8,128)(2,1)} %slope.1.mine_ref, bf16[64,3072]{1,0:T(8,128)(2,1)} %copy-done.3, bf16[64,3072]{1,0:T(8,128)(2,1)} %collective-permute-done.30.before_ref, bf16[64,3072]{1,0:T(8,128)(2,1)} %collective-permute-done.31.after_ref), custom_call_target="tpu_custom_call" | custom-call | flops 1000 | bytes 1000 | tf_op jit(solution)/shard_map/in_order/pallas_call | solution.py:161
  165.9 3.2 %collective-permute-start.33 = (bf16[256,3072]{1,0:T(8,128)(2,1)}, bf16[256,3072]{1,0:T(8,128)(2,1)}, u32[]{:S(2)}, u32[]{:S(2)}) collective-permute-start(bf16[256,3072]{1,0:T(8,128)(2,1)} %in_order.3), channel_id=1, source_target_pairs={{0,3},{1,0},{2,1},{3,2},{4,7},{5,4},{6,5},{7,6},{8,11},{9,8},{10,9... | collective-permute-start | bytes 4718600 | tf_op jit(solution)/shard_map/ppermute | solution.py:264
  172.9 1.4 convolution_dynamic-update-slice_fusion.2
  174.3 20.7 %collective-permute-done.14 = bf16[256,3072]{1,0:T(8,128)(2,1)} collective-permute-done((bf16[256,3072]{1,0:T(8,128)(2,1)}, bf16[256,3072]{1,0:T(8,128)(2,1)}, u32[]{:S(2)}, u32[]{:S(2)}) %collective-permute-start.14) | collective-permute-done | bytes 1572896 | tf_op jit(solution)/shard_map/ppermute | solution.py:264
  195.0 1.2 slice.45
  196.2 1.2 slice.46
  197.5 3.2 %collective-permute-start.17 = (bf16[128,3072]{1,0:T(8,128)(2,1)S(1)}, bf16[128,3072]{1,0:T(8,128)(2,1)S(1)}, u32[]{:S(2)}, u32[]{:S(2)}) collective-permute-start(bf16[128,3072]{1,0:T(8,128)(2,1)S(1)} %slice.46), channel_id=1, source_target_pairs={{0,12},{1,13},{2,14},{3,15},{4,0},{5,1},{6,2},{7,3},{8,4},{9,5},{1... | collective-permute-start | bytes 2359304 | tf_op jit(solution)/shard_map/ppermute | solution.py:264
  200.7 1.9 collective-permute-done.32
  202.6 1.2 slice.53
  203.8 1.2 slice.54
  205.1 3.2 %collective-permute-start.35 = (bf16[128,3072]{1,0:T(8,128)(2,1)S(1)}, bf16[128,3072]{1,0:T(8,128)(2,1)S(1)}, u32[]{:S(2)}, u32[]{:S(2)}) collective-permute-start(bf16[128,3072]{1,0:T(8,128)(2,1)S(1)} %slice.54), channel_id=1, source_target_pairs={{0,3},{1,0},{2,1},{3,2},{4,7},{5,4},{6,5},{7,6},{8,11},{9,8},{10,9... | collective-permute-start | bytes 2359304 | tf_op jit(solution)/shard_map/ppermute | solution.py:264
  208.3 2.9 %convolution_dynamic-update-slice_fusion.1 = f32[1024,768]{1,0:T(8,128)S(1)} fusion(f32[1024,768]{1,0:T(8,128)S(1)} %convolution_dynamic-update-slice_fusion.2, s32[]{:T(128)S(6)} %select_n.37, bf16[256,3072]{1,0:T(8,128)(2,1)} %collective-permute-done.14, bf16[3072,768]{1,0:T(8,128)(2,1)S(1)} %bitcast.71), kind=kOutput, calls=%fused_computation.6 | convolution fusion | flops 1207959552 | bytes 7077892 | tf_op jit(solution)/shard_map/dot_general | solution.py:329
  211.1 2.9 %convolution_dynamic-update-slice_fusion = f32[1024,768]{1,0:T(8,128)S(1)} fusion(f32[1024,768]{1,0:T(8,128)S(1)} %convolution_dynamic-update-slice_fusion.1, s32[]{:T(128)S(6)} %select_n.38, bf16[256,3072]{1,0:T(8,128)(2,1)} %collective-permute-done.15, bf16[3072,768]{1,0:T(8,128)(2,1)S(1)} %bitcast.71), kind=kOutput, calls=%fused_computation.5 | convolution fusion | flops 1207959552 | bytes 7077892 | tf_op jit(solution)/shard_map/dot_general | solution.py:329
  214.0 1.6 constant_dynamic-update-slice_fusion.3
  215.6 1.7 collective-permute-done.16
  217.3 0.8 convolution_dynamic-update-slice_fusion.4
  218.2 0.8 convolution_dynamic-update-slice_fusion.3
  219.2 1.6 constant_dynamic-update-slice_fusion.2
  220.8 2.8 %collective-permute-done.34 = bf16[128,3072]{1,0:T(8,128)(2,1)S(1)} collective-permute-done((bf16[128,3072]{1,0:T(8,128)(2,1)S(1)}, bf16[128,3072]{1,0:T(8,128)(2,1)S(1)}, u32[]{:S(2)}, u32[]{:S(2)}) %collective-permute-start.34) | collective-permute-done | bytes 786464 | tf_op jit(solution)/shard_map/ppermute | solution.py:264
  224.1 2.4 collective-permute-start.21
  226.4 2.2 collective-permute-start.19
  228.7 7.6 %fusion.7 = f32[768,3072]{1,0:T(8,128)} fusion(bf16[1024,768]{1,0:T(8,128)(2,1)S(1)} %bitcast.74, bf16[1024,3072]{1,0:T(8,128)(2,1)S(1)} %constant_dynamic-update-slice_fusion), kind=kOutput, calls=%fused_computation.24 | convolution fusion | flops 4831838208 | bytes 17301504 | tf_op jit(solution)/shard_map/dot_general | solution.py:341
  (58 shorter events, 6.8 us)
Async XLA Ops:
  2.7 13.4 %collective-permute-start.2 = (bf16[256,768]{1,0:T(8,128)(2,1)}, bf16[256,768]{1,0:T(8,128)(2,1)S(1)}, u32[]{:S(2)}, u32[]{:S(2)}) collective-permute-start(bf16[256,768]{1,0:T(8,128)(2,1)} %scale.1), channel_id=1, source_target_pairs={{0,32},{16,48},{32,64},{48,80},{64,96},{80,112},{96,0},{112,16},{1... | collective-permute-start | bytes 1179656 | tf_op jit(solution)/shard_map/ppermute | solution.py:264
  4.7 21.0 %collective-permute-start.1 = (bf16[256,768]{1,0:T(8,128)(2,1)}, bf16[256,768]{1,0:T(8,128)(2,1)S(1)}, u32[]{:S(2)}, u32[]{:S(2)}) collective-permute-start(bf16[256,768]{1,0:T(8,128)(2,1)} %scale.1), channel_id=1, source_target_pairs={{0,64},{16,80},{32,96},{48,112},{64,0},{80,16},{96,32},{112,48},{1... | collective-permute-start | bytes 1179656 | tf_op jit(solution)/shard_map/ppermute | solution.py:264
  8.3 17.5 %collective-permute-start = (bf16[256,768]{1,0:T(8,128)(2,1)}, bf16[256,768]{1,0:T(8,128)(2,1)S(1)}, u32[]{:S(2)}, u32[]{:S(2)}) collective-permute-start(bf16[256,768]{1,0:T(8,128)(2,1)} %scale.1), channel_id=1, source_target_pairs={{0,96},{16,112},{32,0},{48,16},{64,32},{80,48},{96,64},{112,80},{1... | collective-permute-start | bytes 1179656 | tf_op jit(solution)/shard_map/ppermute | solution.py:264
  26.8 3.5 %collective-permute-start.3 = (bf16[1024,768]{1,0:T(8,128)(2,1)S(1)}, bf16[1024,768]{1,0:T(8,128)(2,1)S(1)}, u32[]{:S(2)}, u32[]{:S(2)}) collective-permute-start(bf16[1024,768]{1,0:T(8,128)(2,1)S(1)} %pad_maximum_fusion.1), channel_id=1, source_target_pairs={{0,16},{16,0},{32,48},{48,32},{64,80},{80,64},{96,112},{112,96},{1... | collective-permute-start | bytes 4718600 | tf_op jit(solution)/shard_map/ppermute | solution.py:264
  36.7 28.3 %collective-permute-start.4 = (bf16[256,1536]{1,0:T(8,128)(2,1)}, bf16[256,1536]{1,0:T(8,128)(2,1)}, u32[]{:S(2)}, u32[]{:S(2)}) collective-permute-start(bf16[256,1536]{1,0:T(8,128)(2,1)} %get-tuple-element.63), channel_id=1, source_target_pairs={{0,4},{1,5},{2,6},{3,7},{4,8},{5,9},{6,10},{7,11},{8,12},{9,13},{1... | collective-permute-start | bytes 2359304 | tf_op jit(solution)/shard_map/ppermute | solution.py:264
  38.2 26.8 %collective-permute-start.5 = (bf16[256,1536]{1,0:T(8,128)(2,1)}, bf16[256,1536]{1,0:T(8,128)(2,1)}, u32[]{:S(2)}, u32[]{:S(2)}) collective-permute-start(bf16[256,1536]{1,0:T(8,128)(2,1)} %get-tuple-element.64), channel_id=1, source_target_pairs={{0,12},{1,13},{2,14},{3,15},{4,0},{5,1},{6,2},{7,3},{8,4},{9,5},{1... | collective-permute-start | bytes 2359304 | tf_op jit(solution)/shard_map/ppermute | solution.py:264
  46.4 25.6 %collective-permute-start.22 = (bf16[256,1536]{1,0:T(8,128)(2,1)}, bf16[256,1536]{1,0:T(8,128)(2,1)}, u32[]{:S(2)}, u32[]{:S(2)}) collective-permute-start(bf16[256,1536]{1,0:T(8,128)(2,1)} %get-tuple-element.87), channel_id=1, source_target_pairs={{0,1},{1,2},{2,3},{3,0},{4,5},{5,6},{6,7},{7,4},{8,9},{9,10},{10,1... | collective-permute-start | bytes 2359304 | tf_op jit(solution)/shard_map/ppermute | solution.py:264
  48.0 24.0 %collective-permute-start.23 = (bf16[256,1536]{1,0:T(8,128)(2,1)}, bf16[256,1536]{1,0:T(8,128)(2,1)}, u32[]{:S(2)}, u32[]{:S(2)}) collective-permute-start(bf16[256,1536]{1,0:T(8,128)(2,1)} %get-tuple-element.88), channel_id=1, source_target_pairs={{0,3},{1,0},{2,1},{3,2},{4,7},{5,4},{6,5},{7,6},{8,11},{9,8},{10,9... | collective-permute-start | bytes 2359304 | tf_op jit(solution)/shard_map/ppermute | solution.py:264
  68.7 36.9 %collective-permute-start.6 = (bf16[256,3072]{1,0:T(8,128)(2,1)}, bf16[256,3072]{1,0:T(8,128)(2,1)}, u32[]{:S(2)}, u32[]{:S(2)}) collective-permute-start(bf16[256,3072]{1,0:T(8,128)(2,1)} %get-tuple-element.65), channel_id=1, source_target_pairs={{0,4},{1,5},{2,6},{3,7},{4,8},{5,9},{6,10},{7,11},{8,12},{9,13},{1... | collective-permute-start | bytes 4718600 | tf_op jit(solution)/shard_map/ppermute | solution.py:264
  69.0 36.6 %collective-permute-start.7 = (bf16[256,3072]{1,0:T(8,128)(2,1)}, bf16[256,3072]{1,0:T(8,128)(2,1)}, u32[]{:S(2)}, u32[]{:S(2)}) collective-permute-start(bf16[256,3072]{1,0:T(8,128)(2,1)} %get-tuple-element.66), channel_id=1, source_target_pairs={{0,12},{1,13},{2,14},{3,15},{4,0},{5,1},{6,2},{7,3},{8,4},{9,5},{1... | collective-permute-start | bytes 4718600 | tf_op jit(solution)/shard_map/ppermute | solution.py:264
  75.8 38.7 %collective-permute-start.24 = (bf16[256,3072]{1,0:T(8,128)(2,1)}, bf16[256,3072]{1,0:T(8,128)(2,1)}, u32[]{:S(2)}, u32[]{:S(2)}) collective-permute-start(bf16[256,3072]{1,0:T(8,128)(2,1)} %get-tuple-element.89), channel_id=1, source_target_pairs={{0,1},{1,2},{2,3},{3,0},{4,5},{5,6},{6,7},{7,4},{8,9},{9,10},{10,1... | collective-permute-start | bytes 4718600 | tf_op jit(solution)/shard_map/ppermute | solution.py:264
  76.2 44.3 %collective-permute-start.25 = (bf16[256,3072]{1,0:T(8,128)(2,1)}, bf16[256,3072]{1,0:T(8,128)(2,1)}, u32[]{:S(2)}, u32[]{:S(2)}) collective-permute-start(bf16[256,3072]{1,0:T(8,128)(2,1)} %get-tuple-element.90), channel_id=1, source_target_pairs={{0,3},{1,0},{2,1},{3,2},{4,7},{5,4},{6,5},{7,6},{8,11},{9,8},{10,9... | collective-permute-start | bytes 4718600 | tf_op jit(solution)/shard_map/ppermute | solution.py:264
  109.3 15.0 %collective-permute-start.8 = (bf16[64,3072]{1,0:T(8,128)(2,1)}, bf16[64,3072]{1,0:T(8,128)(2,1)}, u32[]{:S(2)}, u32[]{:S(2)}) collective-permute-start(bf16[64,3072]{1,0:T(8,128)(2,1)} %get-tuple-element.71), channel_id=1, source_target_pairs={{0,2},{1,3},{2,0},{3,1},{4,6},{5,7},{6,4},{7,5},{8,10},{9,11},{10,... | collective-permute-start | bytes 1179656 | tf_op jit(solution)/shard_map/ppermute | solution.py:264
  111.3 17.7 %collective-permute-start.9 = (bf16[64,3072]{1,0:T(8,128)(2,1)}, bf16[64,3072]{1,0:T(8,128)(2,1)}, u32[]{:S(2)}, u32[]{:S(2)}) collective-permute-start(bf16[64,3072]{1,0:T(8,128)(2,1)} %get-tuple-element.72), channel_id=1, source_target_pairs={{0,1},{1,2},{2,3},{3,0},{4,5},{5,6},{6,7},{7,4},{8,9},{9,10},{10,1... | collective-permute-start | bytes 1179656 | tf_op jit(solution)/shard_map/ppermute | solution.py:264
  112.0 17.0 %collective-permute-start.10 = (bf16[64,3072]{1,0:T(8,128)(2,1)}, bf16[64,3072]{1,0:T(8,128)(2,1)}, u32[]{:S(2)}, u32[]{:S(2)}) collective-permute-start(bf16[64,3072]{1,0:T(8,128)(2,1)} %get-tuple-element.73), channel_id=1, source_target_pairs={{0,3},{1,0},{2,1},{3,2},{4,7},{5,4},{6,5},{7,6},{8,11},{9,8},{10,9... | collective-permute-start | bytes 1179656 | tf_op jit(solution)/shard_map/ppermute | solution.py:264
  124.2 12.0 %collective-permute-start.26 = (bf16[64,3072]{1,0:T(8,128)(2,1)}, bf16[64,3072]{1,0:T(8,128)(2,1)S(1)}, u32[]{:S(2)}, u32[]{:S(2)}) collective-permute-start(bf16[64,3072]{1,0:T(8,128)(2,1)} %get-tuple-element.95), channel_id=1, source_target_pairs={{0,8},{1,9},{2,10},{3,11},{4,12},{5,13},{6,14},{7,15},{8,0},{9,1},... | collective-permute-start | bytes 1179656 | tf_op jit(solution)/shard_map/ppermute | solution.py:264
  124.3 13.8 %collective-permute-start.27 = (bf16[64,3072]{1,0:T(8,128)(2,1)}, bf16[64,3072]{1,0:T(8,128)(2,1)}, u32[]{:S(2)}, u32[]{:S(2)}) collective-permute-start(bf16[64,3072]{1,0:T(8,128)(2,1)} %get-tuple-element.96), channel_id=1, source_target_pairs={{0,4},{1,5},{2,6},{3,7},{4,8},{5,9},{6,10},{7,11},{8,12},{9,13},{1... | collective-permute-start | bytes 1179656 | tf_op jit(solution)/shard_map/ppermute | solution.py:264
  124.4 13.7 %collective-permute-start.28 = (bf16[64,3072]{1,0:T(8,128)(2,1)}, bf16[64,3072]{1,0:T(8,128)(2,1)}, u32[]{:S(2)}, u32[]{:S(2)}) collective-permute-start(bf16[64,3072]{1,0:T(8,128)(2,1)} %get-tuple-element.97), channel_id=1, source_target_pairs={{0,12},{1,13},{2,14},{3,15},{4,0},{5,1},{6,2},{7,3},{8,4},{9,5},{1... | collective-permute-start | bytes 1179656 | tf_op jit(solution)/shard_map/ppermute | solution.py:264
  132.4 13.8 %collective-permute-start.11 = (bf16[64,3072]{1,0:T(8,128)(2,1)}, bf16[64,3072]{1,0:T(8,128)(2,1)}, u32[]{:S(2)}, u32[]{:S(2)}) collective-permute-start(bf16[64,3072]{1,0:T(8,128)(2,1)} %get-tuple-element.77.mine_ref), channel_id=1, source_target_pairs={{0,2},{1,3},{2,0},{3,1},{4,6},{5,7},{6,4},{7,5},{8,10},{9,11},{10,... | collective-permute-start | bytes 1179656 | tf_op jit(solution)/shard_map/ppermute | solution.py:264
  134.2 19.6 %collective-permute-start.12 = (bf16[64,3072]{1,0:T(8,128)(2,1)}, bf16[64,3072]{1,0:T(8,128)(2,1)}, u32[]{:S(2)}, u32[]{:S(2)}) collective-permute-start(bf16[64,3072]{1,0:T(8,128)(2,1)} %get-tuple-element.77.mine_ref), channel_id=1, source_target_pairs={{0,1},{1,2},{2,3},{3,0},{4,5},{5,6},{6,7},{7,4},{8,9},{9,10},{10,1... | collective-permute-start | bytes 1179656 | tf_op jit(solution)/shard_map/ppermute | solution.py:264
  136.2 1.8 copy-start.2
  136.2 17.5 %collective-permute-start.13 = (bf16[64,3072]{1,0:T(8,128)(2,1)}, bf16[64,3072]{1,0:T(8,128)(2,1)}, u32[]{:S(2)}, u32[]{:S(2)}) collective-permute-start(bf16[64,3072]{1,0:T(8,128)(2,1)} %get-tuple-element.77.mine_ref), channel_id=1, source_target_pairs={{0,3},{1,0},{2,1},{3,2},{4,7},{5,4},{6,5},{7,6},{8,11},{9,8},{10,9... | collective-permute-start | bytes 1179656 | tf_op jit(solution)/shard_map/ppermute | solution.py:264
  141.8 18.7 %collective-permute-start.29 = (bf16[64,3072]{1,0:T(8,128)(2,1)}, bf16[64,3072]{1,0:T(8,128)(2,1)S(1)}, u32[]{:S(2)}, u32[]{:S(2)}) collective-permute-start(bf16[64,3072]{1,0:T(8,128)(2,1)} %slope.1.mine_ref), channel_id=1, source_target_pairs={{0,8},{1,9},{2,10},{3,11},{4,12},{5,13},{6,14},{7,15},{8,0},{9,1},... | collective-permute-start | bytes 1179656 | tf_op jit(solution)/shard_map/ppermute | solution.py:264
  142.7 18.6 %collective-permute-start.30 = (bf16[64,3072]{1,0:T(8,128)(2,1)}, bf16[64,3072]{1,0:T(8,128)(2,1)}, u32[]{:S(2)}, u32[]{:S(2)}) collective-permute-start(bf16[64,3072]{1,0:T(8,128)(2,1)} %slope.1.mine_ref), channel_id=1, source_target_pairs={{0,4},{1,5},{2,6},{3,7},{4,8},{5,9},{6,10},{7,11},{8,12},{9,13},{1... | collective-permute-start | bytes 1179656 | tf_op jit(solution)/shard_map/ppermute | solution.py:264
  146.3 16.2 %collective-permute-start.31 = (bf16[64,3072]{1,0:T(8,128)(2,1)}, bf16[64,3072]{1,0:T(8,128)(2,1)}, u32[]{:S(2)}, u32[]{:S(2)}) collective-permute-start(bf16[64,3072]{1,0:T(8,128)(2,1)} %slope.1.mine_ref), channel_id=1, source_target_pairs={{0,12},{1,13},{2,14},{3,15},{4,0},{5,1},{6,2},{7,3},{8,4},{9,5},{1... | collective-permute-start | bytes 1179656 | tf_op jit(solution)/shard_map/ppermute | solution.py:264
  157.2 37.8 %collective-permute-start.14 = (bf16[256,3072]{1,0:T(8,128)(2,1)}, bf16[256,3072]{1,0:T(8,128)(2,1)}, u32[]{:S(2)}, u32[]{:S(2)}) collective-permute-start(bf16[256,3072]{1,0:T(8,128)(2,1)} %in_order.2), channel_id=1, source_target_pairs={{0,4},{1,5},{2,6},{3,7},{4,8},{5,9},{6,10},{7,11},{8,12},{9,13},{1... | collective-permute-start | bytes 4718600 | tf_op jit(solution)/shard_map/ppermute | solution.py:264
  157.2 39.0 %collective-permute-start.15 = (bf16[256,3072]{1,0:T(8,128)(2,1)}, bf16[256,3072]{1,0:T(8,128)(2,1)}, u32[]{:S(2)}, u32[]{:S(2)}) collective-permute-start(bf16[256,3072]{1,0:T(8,128)(2,1)} %in_order.2), channel_id=1, source_target_pairs={{0,12},{1,13},{2,14},{3,15},{4,0},{5,1},{6,2},{7,3},{8,4},{9,5},{1... | collective-permute-start | bytes 4718600 | tf_op jit(solution)/shard_map/ppermute | solution.py:264
  160.4 2.0 copy-start.3
  165.9 36.7 %collective-permute-start.32 = (bf16[256,3072]{1,0:T(8,128)(2,1)}, bf16[256,3072]{1,0:T(8,128)(2,1)}, u32[]{:S(2)}, u32[]{:S(2)}) collective-permute-start(bf16[256,3072]{1,0:T(8,128)(2,1)} %in_order.3), channel_id=1, source_target_pairs={{0,1},{1,2},{2,3},{3,0},{4,5},{5,6},{6,7},{7,4},{8,9},{9,10},{10,1... | collective-permute-start | bytes 4718600 | tf_op jit(solution)/shard_map/ppermute | solution.py:264
  165.9 37.9 %collective-permute-start.33 = (bf16[256,3072]{1,0:T(8,128)(2,1)}, bf16[256,3072]{1,0:T(8,128)(2,1)}, u32[]{:S(2)}, u32[]{:S(2)}) collective-permute-start(bf16[256,3072]{1,0:T(8,128)(2,1)} %in_order.3), channel_id=1, source_target_pairs={{0,3},{1,0},{2,1},{3,2},{4,7},{5,4},{6,5},{7,6},{8,11},{9,8},{10,9... | collective-permute-start | bytes 4718600 | tf_op jit(solution)/shard_map/ppermute | solution.py:264
  169.3 2.7 %slice-start = ((s8[4718592]{0:T(1024)(128)(4,1)}), s8[4194304]{0:T(1024)(128)(4,1)S(1)}, s32[]{:S(2)}) async-start(s8[4718592]{0:T(1024)(128)(4,1)} %bitcast.70), calls=%async_computation | async-start | bytes 8388608
  169.5 1.6 copy-start
  169.5 2.6 %slice-start.1 = ((s8[4718592]{0:T(1024)(128)(4,1)}), s8[524288]{0:T(1024)(128)(4,1)S(1)}, s32[]{:S(2)}) async-start(s8[4718592]{0:T(1024)(128)(4,1)} %bitcast.70), calls=%async_computation.1 | async-start | bytes 1048576
  171.0 1.8 copy-start.1
  197.4 19.9 %collective-permute-start.16 = (bf16[128,3072]{1,0:T(8,128)(2,1)S(1)}, bf16[128,3072]{1,0:T(8,128)(2,1)S(1)}, u32[]{:S(2)}, u32[]{:S(2)}) collective-permute-start(bf16[128,3072]{1,0:T(8,128)(2,1)S(1)} %slice.45), channel_id=1, source_target_pairs={{0,4},{1,5},{2,6},{3,7},{4,8},{5,9},{6,10},{7,11},{8,12},{9,13},{1... | collective-permute-start | bytes 2359304 | tf_op jit(solution)/shard_map/ppermute | solution.py:264
  197.5 20.7 %collective-permute-start.17 = (bf16[128,3072]{1,0:T(8,128)(2,1)S(1)}, bf16[128,3072]{1,0:T(8,128)(2,1)S(1)}, u32[]{:S(2)}, u32[]{:S(2)}) collective-permute-start(bf16[128,3072]{1,0:T(8,128)(2,1)S(1)} %slice.46), channel_id=1, source_target_pairs={{0,12},{1,13},{2,14},{3,15},{4,0},{5,1},{6,2},{7,3},{8,4},{9,5},{1... | collective-permute-start | bytes 2359304 | tf_op jit(solution)/shard_map/ppermute | solution.py:264
  205.0 18.6 %collective-permute-start.34 = (bf16[128,3072]{1,0:T(8,128)(2,1)S(1)}, bf16[128,3072]{1,0:T(8,128)(2,1)S(1)}, u32[]{:S(2)}, u32[]{:S(2)}) collective-permute-start(bf16[128,3072]{1,0:T(8,128)(2,1)S(1)} %slice.53), channel_id=1, source_target_pairs={{0,1},{1,2},{2,3},{3,0},{4,5},{5,6},{6,7},{7,4},{8,9},{9,10},{10,1... | collective-permute-start | bytes 2359304 | tf_op jit(solution)/shard_map/ppermute | solution.py:264
  205.1 18.6 %collective-permute-start.35 = (bf16[128,3072]{1,0:T(8,128)(2,1)S(1)}, bf16[128,3072]{1,0:T(8,128)(2,1)S(1)}, u32[]{:S(2)}, u32[]{:S(2)}) collective-permute-start(bf16[128,3072]{1,0:T(8,128)(2,1)S(1)} %slice.54), channel_id=1, source_target_pairs={{0,3},{1,0},{2,1},{3,2},{4,7},{5,4},{6,5},{7,6},{8,11},{9,8},{10,9... | collective-permute-start | bytes 2359304 | tf_op jit(solution)/shard_map/ppermute | solution.py:264
  219.1 4.7 %collective-permute-start.18 = (bf16[512,768]{1,0:T(8,128)(2,1)S(1)}, bf16[512,768]{1,0:T(8,128)(2,1)S(1)}, u32[]{:S(2)}, u32[]{:S(2)}) collective-permute-start(bf16[512,768]{1,0:T(8,128)(2,1)S(1)} %bitcast.76), channel_id=1, source_target_pairs={{0,16},{16,0},{32,48},{48,32},{64,80},{80,64},{96,112},{112,96},{1... | collective-permute-start | bytes 2359304 | tf_op jit(solution)/shard_map/ppermute | solution.py:264
  224.1 12.2 %collective-permute-start.21 = (bf16[128,768]{1,0:T(8,128)(2,1)S(1)}, bf16[128,768]{1,0:T(8,128)(2,1)S(1)}, u32[]{:S(2)}, u32[]{:S(2)}) collective-permute-start(bf16[128,768]{1,0:T(8,128)(2,1)S(1)} %get-tuple-element.84), channel_id=1, source_target_pairs={{0,96},{16,112},{32,0},{48,16},{64,32},{80,48},{96,64},{112,80},{1... | collective-permute-start | bytes 589832 | tf_op jit(solution)/shard_map/ppermute | solution.py:264
  226.4 9.8 %collective-permute-start.20 = (bf16[128,768]{1,0:T(8,128)(2,1)S(1)}, bf16[128,768]{1,0:T(8,128)(2,1)S(1)}, u32[]{:S(2)}, u32[]{:S(2)}) collective-permute-start(bf16[128,768]{1,0:T(8,128)(2,1)S(1)} %get-tuple-element.83), channel_id=1, source_target_pairs={{0,32},{16,48},{32,64},{48,80},{64,96},{80,112},{96,0},{112,16},{1... | collective-permute-start | bytes 589832 | tf_op jit(solution)/shard_map/ppermute | solution.py:264
  226.4 9.8 %collective-permute-start.19 = (bf16[128,768]{1,0:T(8,128)(2,1)S(1)}, bf16[128,768]{1,0:T(8,128)(2,1)S(1)}, u32[]{:S(2)}, u32[]{:S(2)}) collective-permute-start(bf16[128,768]{1,0:T(8,128)(2,1)S(1)} %get-tuple-element.82), channel_id=1, source_target_pairs={{0,64},{16,80},{32,96},{48,112},{64,0},{80,16},{96,32},{112,48},{1... | collective-permute-start | bytes 589832 | tf_op jit(solution)/shard_map/ppermute | solution.py:264

commit v2 on v1

--- a/solution.py
+++ b/solution.py
@@ -13,6 +13,7 @@
 PIECES = 3
 BF16 = jnp.bfloat16
 F32 = jnp.float32
+SMALL = pltpu.CompilerParams(vmem_limit_bytes=10 * 1024 * 1024)
 COST = pl.CostEstimate(flops=1000, bytes_accessed=1000, transcendentals=0)
 
 
@@ -112,6 +113,7 @@
         blocks_kernel,
         grid_spec=grid,
         out_shape=[pltpu.HBM((big // SIDE, units), kind) for kind in (BF16, BF16, BF16, F32)],
+        compiler_params=SMALL,
         cost_estimate=COST,
         name="row_blocks",
     )(place.reshape(1), *(list(terms) * SIDE))
@@ -137,6 +139,7 @@
         in_specs=[spec] * len(ins),
         out_specs=[spec] * len(kinds),
         out_shape=[jax.ShapeDtypeStruct((rows_in, units), kind) for kind in kinds],
+        compiler_params=SMALL,
         cost_estimate=COST,
         name=name,
     )(*ins)
@@ -162,6 +165,7 @@
         put_kernel,
         grid_spec=grid,
         out_shape=jax.ShapeDtypeStruct((SIDE * small, units), BF16),
+        compiler_params=SMALL,
         cost_estimate=COST,
         name="in_order",
     )(place.reshape(1), *blocks)
@@ -209,7 +213,7 @@
             functools.partial(kernel, self.tensor),
             grid_spec=grid,
             out_shape=outs,
-            compiler_params=pltpu.CompilerParams(vmem_limit_bytes=24 * 1024 * 1024),
+            compiler_params=pltpu.CompilerParams(vmem_limit_bytes=16 * 1024 * 1024),
             cost_estimate=COST,
             name=name,
         )(place.reshape(1), *(held * len(steps)), *([in_hbm(self.weight)] * PIECES))
@@ -245,6 +249,7 @@
             grid_spec=grid,
             out_shape=[pltpu.HBM(after.shape, BF16)] * 2,
             input_output_aliases={1: 0, 2: 1},
+            compiler_params=SMALL,
             cost_estimate=COST,
             name="add_far",
         )(place.reshape(1), in_hbm(after), in_hbm(before), *got)

time: 240 us -> 232 us (0.967)
  Pallas kernels: 59.2 us -> 46.7 us
  starting transfers between devices: 56.7 us -> 63.3 us
  waiting for transfers between devices: 89.8 us -> 87.3 us
    ppermute x36, starting transfers between devices: 56.7 us -> 63.3 us  [send(): lax.ppermute(a, 'col' if axis in ('x', 'y') else 'row', steps_on(axis, st...]
    pallas_call x2, Pallas kernels: 7.09 us -> 1.73 us  [by_tiles(): pl.pallas_call(kernel, grid=(3,), in_specs=[spec] * len(ins), out_specs=[...]
    pallas_call x2, Pallas kernels: 6.89 us -> 3.59 us  [in_order(): pl.pallas_call(put_kernel, grid_spec=grid, out_shape=jax.ShapeDtypeStruct...]
    pallas_call x2, Pallas kernels: 7.42 us -> 4.33 us  [row_blocks(): pl.pallas_call(blocks_kernel, grid_spec=grid, out_shape=[pltpu.HBM((big /...]
    ppermute x36, waiting for transfers between devices: 89.8 us -> 87.3 us  [send(): lax.ppermute(a, 'col' if axis in ('x', 'y') else 'row', steps_on(axis, st...]
  transfers between devices with their start and end apart: 36 -> 36, of which waited for: 14 -> 16; matrix products, arithmetic and copies ran while one was open for 11% -> 13% of each run, Pallas kernels for 21% -> 17%
where the time goes in v2:
time: 232 us; the launch traced here: 231 us
  waiting for transfers between devices  87.3 us (38%)
  starting transfers between devices  63.3 us (27%)
  Pallas kernels  46.7 us (20%)
  matrix products  17.8 us (8%)
  local copies, waits for them, and re-layouts  12.5 us (5%)
    ppermute x36, waiting for transfers between devices, send(): lax.ppermute(a, 'col' if axis in ('x', 'y') else 'row', steps_on(axis, st...  87.3 us
    ppermute x36, starting transfers between devices, send(): lax.ppermute(a, 'col' if axis in ('x', 'y') else 'row', steps_on(axis, st...  63.3 us
    pallas_call x4, Pallas kernels, call(): pl.pallas_call(functools.partial(kernel, self.tensor), grid_spec=grid, ou...  28.1 us
    dot_general x5, matrix products, local(): term = jnp.dot(block, down_weight, preferred_element_type=F32)  10.3 us
    dot_general x1, matrix products, local(): lax.dot_general(crossed, whole, (((0,), (0,)), ((), ())), preferred_eleme...  7.54 us
    pallas_call x2, Pallas kernels, add(): pl.pallas_call(add_kernel, grid_spec=grid, out_shape=[pltpu.HBM(after.sha...  6.9 us
    dynamic_update_slice x5, local copies, waits for them, and re-layouts, local(): lax.dynamic_update_slice_in_dim(whole, block, lax.rem(slot, SIDE) * big +...  5.37 us
    slice x4, local copies, waits for them, and re-layouts, wide_gather(): far = trade((before[:n], axis, 1), (after[n:], axis, -1))  4.74 us
  transfers between devices with their start and end apart: 36, of which 16 were waited for; matrix products, arithmetic and copies ran while one was open for 13% of the time, Pallas kernels for 17%

profile of v2, /device:TPU:0, one launch (start us, length us, event | category | flops | bytes accessed | tf_op | source)
XLA Modules:
  0.0 230.8 jit_solution(18368902085148637076)
XLA Ops:
  0.6 2.0 scale.1
  2.7 2.0 collective-permute-start.2
  4.7 3.6 %collective-permute-start.1 = (bf16[256,768]{1,0:T(8,128)(2,1)}, bf16[256,768]{1,0:T(8,128)(2,1)S(1)}, u32[]{:S(2)}, u32[]{:S(2)}) collective-permute-start(bf16[256,768]{1,0:T(8,128)(2,1)} %scale.1), channel_id=1, source_target_pairs={{0,64},{16,80},{32,96},{48,112},{64,0},{80,16},{96,32},{112,48},{1... | collective-permute-start | bytes 1179656 | tf_op jit(solution)/shard_map/ppermute | solution.py:269
  8.3 1.0 collective-permute-start
  9.3 6.9 %collective-permute-done.2 = bf16[256,768]{1,0:T(8,128)(2,1)S(1)} collective-permute-done((bf16[256,768]{1,0:T(8,128)(2,1)}, bf16[256,768]{1,0:T(8,128)(2,1)S(1)}, u32[]{:S(2)}, u32[]{:S(2)}) %collective-permute-start.2) | collective-permute-done | bytes 393248 | tf_op jit(solution)/shard_map/ppermute | solution.py:269
  16.1 9.6 %collective-permute-done.1 = bf16[256,768]{1,0:T(8,128)(2,1)S(1)} collective-permute-done((bf16[256,768]{1,0:T(8,128)(2,1)}, bf16[256,768]{1,0:T(8,128)(2,1)S(1)}, u32[]{:S(2)}, u32[]{:S(2)}) %collective-permute-start.1) | collective-permute-done | bytes 393248 | tf_op jit(solution)/shard_map/ppermute | solution.py:269
  25.7 1.1 pad_maximum_fusion.1
  26.9 3.4 %collective-permute-done.3 = bf16[1024,768]{1,0:T(8,128)(2,1)S(1)} collective-permute-done((bf16[1024,768]{1,0:T(8,128)(2,1)S(1)}, bf16[1024,768]{1,0:T(8,128)(2,1)S(1)}, u32[]{:S(2)}, u32[]{:S(2)}) %collective-permute-start.3) | collective-permute-done | bytes 1572896 | tf_op jit(solution)/shard_map/ppermute | solution.py:269
  30.3 6.3 %far_share.2 = (bf16[256,1536]{1,0:T(8,128)(2,1)}, bf16[256,1536]{1,0:T(8,128)(2,1)}) custom-call(s32[1]{0:T(128)} %bitcast.6.slot_ref, bf16[4,2,2,64,768]{4,3,2,1,0:T(8,128)(2,1)S(1)} %bitcast.52, bf16[4,2,2,64,768]{4,3,2,1,0:T(8,128)(2,1)S(1)} %bitcast.61, bf16[768,3072]{1,0:T(8,128)(2,1)} %refs_2_.2, bf16[768,3072]{1,0:T(8,128)(2,1)} %refs_2_.2, ...), custom_call_target="tpu_custom_call" | custom-call | flops 1000 | bytes 1000 | tf_op jit(solution)/shard_map/far_share/pallas_call | solution.py:212
  36.6 1.5 collective-permute-start.4
  38.1 1.7 collective-permute-start.5
  39.9 6.5 %far_share.3 = (bf16[256,1536]{1,0:T(8,128)(2,1)}, bf16[256,1536]{1,0:T(8,128)(2,1)}) custom-call(s32[1]{0:T(128)} %bitcast.20.slot_ref, bf16[4,2,2,64,768]{4,3,2,1,0:T(8,128)(2,1)S(1)} %bitcast.53, bf16[4,2,2,64,768]{4,3,2,1,0:T(8,128)(2,1)S(1)} %bitcast.62, bf16[3072,768]{1,0:T(8,128)(2,1)} %refs_2_.3, bf16[3072,768]{1,0:T(8,128)(2,1)} %refs_2_.3, ...), custom_call_target="tpu_custom_call" | custom-call | flops 1000 | bytes 1000 | tf_op jit(solution)/shard_map/far_share/pallas_call | solution.py:212
  46.4 1.6 collective-permute-start.22
  47.9 1.7 collective-permute-start.23
  49.6 7.5 %near_shares.2 = (bf16[256,3072]{1,0:T(8,128)(2,1)}, bf16[256,3072]{1,0:T(8,128)(2,1)}, bf16[256,3072]{1,0:T(8,128)(2,1)}) custom-call(s32[1]{0:T(128)} %bitcast.1.slot_ref, bf16[4,2,2,64,768]{4,3,2,1,0:T(8,128)(2,1)S(1)} %bitcast.54, bf16[4,2,2,64,768]{4,3,2,1,0:T(8,128)(2,1)S(1)} %bitcast.63, bf16[4,2,2,64,768]{4,3,2,1,0:T(8,128)(2,1)S(1)} %bitcast.55, ...), custom_call_target="tpu_custom_call" | custom-call | flops 1000 | bytes 1000 | tf_op jit(solution)/shard_map/near_shares/pallas_call | solution.py:212
  57.1 7.8 %near_shares.3 = (bf16[256,3072]{1,0:T(8,128)(2,1)}, bf16[256,3072]{1,0:T(8,128)(2,1)}, bf16[256,3072]{1,0:T(8,128)(2,1)}) custom-call(s32[1]{0:T(128)} %bitcast.4.slot_ref, bf16[4,2,2,64,768]{4,3,2,1,0:T(8,128)(2,1)S(1)} %bitcast.57, bf16[4,2,2,64,768]{4,3,2,1,0:T(8,128)(2,1)S(1)} %bitcast.66, bf16[4,2,2,64,768]{4,3,2,1,0:T(8,128)(2,1)S(1)} %bitcast.58, ...), custom_call_target="tpu_custom_call" | custom-call | flops 1000 | bytes 1000 | tf_op jit(solution)/shard_map/near_shares/pallas_call | solution.py:212
  64.9 3.4 %add_far.2 = (bf16[256,3072]{1,0:T(8,128)(2,1)}, bf16[256,3072]{1,0:T(8,128)(2,1)}) custom-call(s32[1]{0:T(128)} %bitcast.5.slot_ref, bf16[256,3072]{1,0:T(8,128)(2,1)} %get-tuple-element.61.after_ref, bf16[256,3072]{1,0:T(8,128)(2,1)} %get-tuple-element.62.before_ref, ...), custom_call_target="tpu_custom_call", output_to_operand_aliasing={{0}: (1, {}), {1}: (2, {})} | custom-call | flops 1000 | bytes 1000 | tf_op jit(solution)/shard_map/add_far/pallas_call | solution.py:247
  68.7 3.0 %collective-permute-start.7 = (bf16[256,3072]{1,0:T(8,128)(2,1)}, bf16[256,3072]{1,0:T(8,128)(2,1)S(1)}, u32[]{:S(2)}, u32[]{:S(2)}) collective-permute-start(bf16[256,3072]{1,0:T(8,128)(2,1)} %get-tuple-element.66), channel_id=1, source_target_pairs={{0,12},{1,13},{2,14},{3,15},{4,0},{5,1},{6,2},{7,3},{8,4},{9,5},{1... | collective-permute-start | bytes 4718600 | tf_op jit(solution)/shard_map/ppermute | solution.py:269
  71.6 3.5 %add_far.3 = (bf16[256,3072]{1,0:T(8,128)(2,1)}, bf16[256,3072]{1,0:T(8,128)(2,1)}) custom-call(s32[1]{0:T(128)} %bitcast.20.slot_ref, bf16[256,3072]{1,0:T(8,128)(2,1)} %get-tuple-element.85.after_ref, bf16[256,3072]{1,0:T(8,128)(2,1)} %get-tuple-element.86.before_ref, ...), custom_call_target="tpu_custom_call", output_to_operand_aliasing={{0}: (1, {}), {1}: (2, {})} | custom-call | flops 1000 | bytes 1000 | tf_op jit(solution)/shard_map/add_far/pallas_call | solution.py:247
  75.5 2.9 %collective-permute-start.25 = (bf16[256,3072]{1,0:T(8,128)(2,1)}, bf16[256,3072]{1,0:T(8,128)(2,1)S(1)}, u32[]{:S(2)}, u32[]{:S(2)}) collective-permute-start(bf16[256,3072]{1,0:T(8,128)(2,1)} %get-tuple-element.90), channel_id=1, source_target_pairs={{0,3},{1,0},{2,1},{3,2},{4,7},{5,4},{6,5},{7,6},{8,11},{9,8},{10,9... | collective-permute-start | bytes 4718600 | tf_op jit(solution)/shard_map/ppermute | solution.py:269
  78.3 26.9 %collective-permute-done.6.refs_1_.refs_4_.refs_7_.refs_10_ = bf16[256,3072]{1,0:T(8,128)(2,1)S(1)} collective-permute-done((bf16[256,3072]{1,0:T(8,128)(2,1)}, bf16[256,3072]{1,0:T(8,128)(2,1)S(1)}, u32[]{:S(2)}, u32[]{:S(2)}) %collective-permute-start.6) | collective-permute-done | bytes 1572896 | tf_op jit(solution)/shard_map/ppermute | solution.py:269
  105.2 2.2 row_blocks.2
  107.4 1.9 collective-permute-start.8
  110.0 2.6 %collective-permute-start.10 = (bf16[64,3072]{1,0:T(8,128)(2,1)}, bf16[64,3072]{1,0:T(8,128)(2,1)S(1)}, u32[]{:S(2)}, u32[]{:S(2)}) collective-permute-start(bf16[64,3072]{1,0:T(8,128)(2,1)} %get-tuple-element.73), channel_id=1, source_target_pairs={{0,3},{1,0},{2,1},{3,2},{4,7},{5,4},{6,5},{7,6},{8,11},{9,8},{10,9... | collective-permute-start | bytes 1179656 | tf_op jit(solution)/shard_map/ppermute | solution.py:269
  112.5 7.3 %collective-permute-done.24.refs_1_.refs_4_.refs_7_.refs_10_ = bf16[256,3072]{1,0:T(8,128)(2,1)S(1)} collective-permute-done((bf16[256,3072]{1,0:T(8,128)(2,1)}, bf16[256,3072]{1,0:T(8,128)(2,1)S(1)}, u32[]{:S(2)}, u32[]{:S(2)}) %collective-permute-start.24) | collective-permute-done | bytes 1572896 | tf_op jit(solution)/shard_map/ppermute | solution.py:269
  120.3 2.1 row_blocks.3
  122.9 3.2 %collective-permute-start.28 = (bf16[64,3072]{1,0:T(8,128)(2,1)}, bf16[64,3072]{1,0:T(8,128)(2,1)S(1)}, u32[]{:S(2)}, u32[]{:S(2)}) collective-permute-start(bf16[64,3072]{1,0:T(8,128)(2,1)} %get-tuple-element.97), channel_id=1, source_target_pairs={{0,12},{1,13},{2,14},{3,15},{4,0},{5,1},{6,2},{7,3},{8,4},{9,5},{1... | collective-permute-start | bytes 1179656 | tf_op jit(solution)/shard_map/ppermute | solution.py:269
  126.2 2.0 collective-permute-done.9.c_ref
  128.9 1.8 collective-permute-start.11
  130.7 2.0 collective-permute-start.12
  132.8 3.0 %collective-permute-start.13 = (bf16[64,3072]{1,0:T(8,128)(2,1)S(1)}, bf16[64,3072]{1,0:T(8,128)(2,1)S(1)}, u32[]{:S(2)}, u32[]{:S(2)}) collective-permute-start(bf16[64,3072]{1,0:T(8,128)(2,1)S(1)} %get-tuple-element.77.mine_ref), channel_id=1, source_target_pairs={{0,3},{1,0},{2,1},{3,2},{4,7},{5,4},{6,5},{7,6},{8,11},{9,8},{10,9... | collective-permute-start | bytes 1179656 | tf_op jit(solution)/shard_map/ppermute | solution.py:269
  136.2 1.1 copy-done.2
  137.3 1.0 slope.1.mine_ref
  138.9 1.0 collective-permute-start.30
  139.9 2.6 %collective-permute-done.11.far_ref = bf16[64,3072]{1,0:T(8,128)(2,1)S(1)} collective-permute-done((bf16[64,3072]{1,0:T(8,128)(2,1)S(1)}, bf16[64,3072]{1,0:T(8,128)(2,1)S(1)}, u32[]{:S(2)}, u32[]{:S(2)}) %collective-permute-start.11) | collective-permute-done | bytes 393248 | tf_op jit(solution)/shard_map/ppermute | solution.py:269
  142.6 1.1 collective-permute-start.31
  143.7 5.6 %collective-permute-done.12.before_ref = bf16[64,3072]{1,0:T(8,128)(2,1)S(1)} collective-permute-done((bf16[64,3072]{1,0:T(8,128)(2,1)S(1)}, bf16[64,3072]{1,0:T(8,128)(2,1)S(1)}, u32[]{:S(2)}, u32[]{:S(2)}) %collective-permute-start.12) | collective-permute-done | bytes 393248 | tf_op jit(solution)/shard_map/ppermute | solution.py:269
  149.3 1.8 in_order.2
  151.1 3.2 %collective-permute-start.15 = (bf16[256,3072]{1,0:T(8,128)(2,1)}, bf16[256,3072]{1,0:T(8,128)(2,1)}, u32[]{:S(2)}, u32[]{:S(2)}) collective-permute-start(bf16[256,3072]{1,0:T(8,128)(2,1)} %in_order.2), channel_id=1, source_target_pairs={{0,12},{1,13},{2,14},{3,15},{4,0},{5,1},{6,2},{7,3},{8,4},{9,5},{1... | collective-permute-start | bytes 4718600 | tf_op jit(solution)/shard_map/ppermute | solution.py:269
  155.5 1.8 in_order.3
  157.9 7.8 %collective-permute-start.33 = (bf16[256,3072]{1,0:T(8,128)(2,1)}, bf16[256,3072]{1,0:T(8,128)(2,1)}, u32[]{:S(2)}, u32[]{:S(2)}) collective-permute-start(bf16[256,3072]{1,0:T(8,128)(2,1)} %in_order.3), channel_id=1, source_target_pairs={{0,3},{1,0},{2,1},{3,2},{4,7},{5,4},{6,5},{7,6},{8,11},{9,8},{10,9... | collective-permute-start | bytes 4718600 | tf_op jit(solution)/shard_map/ppermute | solution.py:269
  166.0 0.8 broadcast_in_dim.7
  166.8 2.0 constant_dynamic-update-slice_fusion.4
  169.1 2.9 %convolution_dynamic-update-slice_fusion.2 = f32[1024,768]{1,0:T(8,128)S(1)} fusion(f32[1024,768]{1,0:T(8,128)S(1)} %broadcast_in_dim.6, s32[]{:T(128)S(6)} %select_n.36, bf16[256,3072]{1,0:T(8,128)(2,1)} %in_order.2, bf16[3072,768]{1,0:T(8,128)(2,1)S(1)} %bitcast.71), kind=kOutput, calls=%fused_computation.7 | convolution fusion | flops 1207959552 | bytes 7077892 | tf_op jit(solution)/shard_map/dot_general | solution.py:334
  171.9 16.9 %collective-permute-done.14 = bf16[256,3072]{1,0:T(8,128)(2,1)} collective-permute-done((bf16[256,3072]{1,0:T(8,128)(2,1)}, bf16[256,3072]{1,0:T(8,128)(2,1)}, u32[]{:S(2)}, u32[]{:S(2)}) %collective-permute-start.14) | collective-permute-done | bytes 1572896 | tf_op jit(solution)/shard_map/ppermute | solution.py:269
  188.9 1.2 slice.45
  190.1 1.2 slice.46
  191.4 3.2 %collective-permute-start.17 = (bf16[128,3072]{1,0:T(8,128)(2,1)S(1)}, bf16[128,3072]{1,0:T(8,128)(2,1)S(1)}, u32[]{:S(2)}, u32[]{:S(2)}) collective-permute-start(bf16[128,3072]{1,0:T(8,128)(2,1)S(1)} %slice.46), channel_id=1, source_target_pairs={{0,12},{1,13},{2,14},{3,15},{4,0},{5,1},{6,2},{7,3},{8,4},{9,5},{1... | collective-permute-start | bytes 2359304 | tf_op jit(solution)/shard_map/ppermute | solution.py:269
  194.6 1.2 slice.53
  195.8 1.2 slice.54
  197.0 0.9 collective-permute-start.34
  197.9 4.8 %collective-permute-start.35 = (bf16[128,3072]{1,0:T(8,128)(2,1)S(1)}, bf16[128,3072]{1,0:T(8,128)(2,1)S(1)}, u32[]{:S(2)}, u32[]{:S(2)}) collective-permute-start(bf16[128,3072]{1,0:T(8,128)(2,1)S(1)} %slice.54), channel_id=1, source_target_pairs={{0,3},{1,0},{2,1},{3,2},{4,7},{5,4},{6,5},{7,6},{8,11},{9,8},{10,9... | collective-permute-start | bytes 2359304 | tf_op jit(solution)/shard_map/ppermute | solution.py:269
  202.7 2.9 %convolution_dynamic-update-slice_fusion.1 = f32[1024,768]{1,0:T(8,128)S(1)} fusion(f32[1024,768]{1,0:T(8,128)S(1)} %convolution_dynamic-update-slice_fusion.2, s32[]{:T(128)S(6)} %select_n.37, bf16[256,3072]{1,0:T(8,128)(2,1)} %collective-permute-done.14, bf16[3072,768]{1,0:T(8,128)(2,1)S(1)} %bitcast.71), kind=kOutput, calls=%fused_computation.6 | convolution fusion | flops 1207959552 | bytes 7077892 | tf_op jit(solution)/shard_map/dot_general | solution.py:334
  205.6 2.9 %convolution_dynamic-update-slice_fusion = f32[1024,768]{1,0:T(8,128)S(1)} fusion(f32[1024,768]{1,0:T(8,128)S(1)} %convolution_dynamic-update-slice_fusion.1, s32[]{:T(128)S(6)} %select_n.38, bf16[256,3072]{1,0:T(8,128)(2,1)} %collective-permute-done.15, bf16[3072,768]{1,0:T(8,128)(2,1)S(1)} %bitcast.71), kind=kOutput, calls=%fused_computation.5 | convolution fusion | flops 1207959552 | bytes 7077892 | tf_op jit(solution)/shard_map/dot_general | solution.py:334
  208.4 1.6 constant_dynamic-update-slice_fusion.3
  210.1 1.1 collective-permute-done.16
  211.2 0.8 convolution_dynamic-update-slice_fusion.4
  212.0 0.9 convolution_dynamic-update-slice_fusion.3
  213.1 1.6 constant_dynamic-update-slice_fusion.2
  214.7 2.0 collective-permute-done.34
  217.2 2.3 %collective-permute-start.21 = (bf16[128,768]{1,0:T(8,128)(2,1)S(1)}, bf16[128,768]{1,0:T(8,128)(2,1)S(1)}, u32[]{:S(2)}, u32[]{:S(2)}) collective-permute-start(bf16[128,768]{1,0:T(8,128)(2,1)S(1)} %get-tuple-element.84), channel_id=1, source_target_pairs={{0,96},{16,112},{32,0},{48,16},{64,32},{80,48},{96,64},{112,80},{1... | collective-permute-start | bytes 589832 | tf_op jit(solution)/shard_map/ppermute | solution.py:269
  219.5 2.2 collective-permute-start.19
  221.7 7.5 %fusion.7 = f32[768,3072]{1,0:T(8,128)} fusion(bf16[1024,768]{1,0:T(8,128)(2,1)S(1)} %bitcast.74, bf16[1024,3072]{1,0:T(8,128)(2,1)S(1)} %constant_dynamic-update-slice_fusion), kind=kOutput, calls=%fused_computation.24 | convolution fusion | flops 4831838208 | bytes 17301504 | tf_op jit(solution)/shard_map/dot_general | solution.py:346
  229.2 0.8 collective-permute-done.20
  (58 shorter events, 7.7 us)
Async XLA Ops:
  2.7 13.4 %collective-permute-start.2 = (bf16[256,768]{1,0:T(8,128)(2,1)}, bf16[256,768]{1,0:T(8,128)(2,1)S(1)}, u32[]{:S(2)}, u32[]{:S(2)}) collective-permute-start(bf16[256,768]{1,0:T(8,128)(2,1)} %scale.1), channel_id=1, source_target_pairs={{0,32},{16,48},{32,64},{48,80},{64,96},{80,112},{96,0},{112,16},{1... | collective-permute-start | bytes 1179656 | tf_op jit(solution)/shard_map/ppermute | solution.py:269
  4.7 21.0 %collective-permute-start.1 = (bf16[256,768]{1,0:T(8,128)(2,1)}, bf16[256,768]{1,0:T(8,128)(2,1)S(1)}, u32[]{:S(2)}, u32[]{:S(2)}) collective-permute-start(bf16[256,768]{1,0:T(8,128)(2,1)} %scale.1), channel_id=1, source_target_pairs={{0,64},{16,80},{32,96},{48,112},{64,0},{80,16},{96,32},{112,48},{1... | collective-permute-start | bytes 1179656 | tf_op jit(solution)/shard_map/ppermute | solution.py:269
  8.3 17.5 %collective-permute-start = (bf16[256,768]{1,0:T(8,128)(2,1)}, bf16[256,768]{1,0:T(8,128)(2,1)S(1)}, u32[]{:S(2)}, u32[]{:S(2)}) collective-permute-start(bf16[256,768]{1,0:T(8,128)(2,1)} %scale.1), channel_id=1, source_target_pairs={{0,96},{16,112},{32,0},{48,16},{64,32},{80,48},{96,64},{112,80},{1... | collective-permute-start | bytes 1179656 | tf_op jit(solution)/shard_map/ppermute | solution.py:269
  26.8 3.5 %collective-permute-start.3 = (bf16[1024,768]{1,0:T(8,128)(2,1)S(1)}, bf16[1024,768]{1,0:T(8,128)(2,1)S(1)}, u32[]{:S(2)}, u32[]{:S(2)}) collective-permute-start(bf16[1024,768]{1,0:T(8,128)(2,1)S(1)} %pad_maximum_fusion.1), channel_id=1, source_target_pairs={{0,16},{16,0},{32,48},{48,32},{64,80},{80,64},{96,112},{112,96},{1... | collective-permute-start | bytes 4718600 | tf_op jit(solution)/shard_map/ppermute | solution.py:269
  36.6 28.3 %collective-permute-start.4 = (bf16[256,1536]{1,0:T(8,128)(2,1)}, bf16[256,1536]{1,0:T(8,128)(2,1)S(1)}, u32[]{:S(2)}, u32[]{:S(2)}) collective-permute-start(bf16[256,1536]{1,0:T(8,128)(2,1)} %get-tuple-element.63), channel_id=1, source_target_pairs={{0,4},{1,5},{2,6},{3,7},{4,8},{5,9},{6,10},{7,11},{8,12},{9,13},{1... | collective-permute-start | bytes 2359304 | tf_op jit(solution)/shard_map/ppermute | solution.py:269
  38.1 26.8 %collective-permute-start.5 = (bf16[256,1536]{1,0:T(8,128)(2,1)}, bf16[256,1536]{1,0:T(8,128)(2,1)S(1)}, u32[]{:S(2)}, u32[]{:S(2)}) collective-permute-start(bf16[256,1536]{1,0:T(8,128)(2,1)} %get-tuple-element.64), channel_id=1, source_target_pairs={{0,12},{1,13},{2,14},{3,15},{4,0},{5,1},{6,2},{7,3},{8,4},{9,5},{1... | collective-permute-start | bytes 2359304 | tf_op jit(solution)/shard_map/ppermute | solution.py:269
  46.4 25.3 %collective-permute-start.22 = (bf16[256,1536]{1,0:T(8,128)(2,1)}, bf16[256,1536]{1,0:T(8,128)(2,1)S(1)}, u32[]{:S(2)}, u32[]{:S(2)}) collective-permute-start(bf16[256,1536]{1,0:T(8,128)(2,1)} %get-tuple-element.87), channel_id=1, source_target_pairs={{0,1},{1,2},{2,3},{3,0},{4,5},{5,6},{6,7},{7,4},{8,9},{9,10},{10,1... | collective-permute-start | bytes 2359304 | tf_op jit(solution)/shard_map/ppermute | solution.py:269
  47.9 23.7 %collective-permute-start.23 = (bf16[256,1536]{1,0:T(8,128)(2,1)}, bf16[256,1536]{1,0:T(8,128)(2,1)S(1)}, u32[]{:S(2)}, u32[]{:S(2)}) collective-permute-start(bf16[256,1536]{1,0:T(8,128)(2,1)} %get-tuple-element.88), channel_id=1, source_target_pairs={{0,3},{1,0},{2,1},{3,2},{4,7},{5,4},{6,5},{7,6},{8,11},{9,8},{10,9... | collective-permute-start | bytes 2359304 | tf_op jit(solution)/shard_map/ppermute | solution.py:269
  68.4 36.8 %copy-start.1 = (bf16[256,3072]{1,0:T(8,128)(2,1)S(1)}, bf16[256,3072]{1,0:T(8,128)(2,1)}, u32[]{:S(2)}) copy-start(bf16[256,3072]{1,0:T(8,128)(2,1)} %get-tuple-element.57.refs_0_.refs_3_.refs_6_.refs_9_) | copy-start | bytes 4718596
  68.4 36.8 %collective-permute-start.6 = (bf16[256,3072]{1,0:T(8,128)(2,1)}, bf16[256,3072]{1,0:T(8,128)(2,1)S(1)}, u32[]{:S(2)}, u32[]{:S(2)}) collective-permute-start(bf16[256,3072]{1,0:T(8,128)(2,1)} %get-tuple-element.65), channel_id=1, source_target_pairs={{0,4},{1,5},{2,6},{3,7},{4,8},{5,9},{6,10},{7,11},{8,12},{9,13},{1... | collective-permute-start | bytes 4718600 | tf_op jit(solution)/shard_map/ppermute | solution.py:269
  68.7 36.5 %collective-permute-start.7 = (bf16[256,3072]{1,0:T(8,128)(2,1)}, bf16[256,3072]{1,0:T(8,128)(2,1)S(1)}, u32[]{:S(2)}, u32[]{:S(2)}) collective-permute-start(bf16[256,3072]{1,0:T(8,128)(2,1)} %get-tuple-element.66), channel_id=1, source_target_pairs={{0,12},{1,13},{2,14},{3,15},{4,0},{5,1},{6,2},{7,3},{8,4},{9,5},{1... | collective-permute-start | bytes 4718600 | tf_op jit(solution)/shard_map/ppermute | solution.py:269
  75.1 44.7 %collective-permute-start.24 = (bf16[256,3072]{1,0:T(8,128)(2,1)}, bf16[256,3072]{1,0:T(8,128)(2,1)S(1)}, u32[]{:S(2)}, u32[]{:S(2)}) collective-permute-start(bf16[256,3072]{1,0:T(8,128)(2,1)} %get-tuple-element.89), channel_id=1, source_target_pairs={{0,1},{1,2},{2,3},{3,0},{4,5},{5,6},{6,7},{7,4},{8,9},{9,10},{10,1... | collective-permute-start | bytes 4718600 | tf_op jit(solution)/shard_map/ppermute | solution.py:269
  75.5 44.9 %collective-permute-start.25 = (bf16[256,3072]{1,0:T(8,128)(2,1)}, bf16[256,3072]{1,0:T(8,128)(2,1)S(1)}, u32[]{:S(2)}, u32[]{:S(2)}) collective-permute-start(bf16[256,3072]{1,0:T(8,128)(2,1)} %get-tuple-element.90), channel_id=1, source_target_pairs={{0,3},{1,0},{2,1},{3,2},{4,7},{5,4},{6,5},{7,6},{8,11},{9,8},{10,9... | collective-permute-start | bytes 4718600 | tf_op jit(solution)/shard_map/ppermute | solution.py:269
  105.2 15.1 %copy-start = (bf16[256,3072]{1,0:T(8,128)(2,1)S(1)}, bf16[256,3072]{1,0:T(8,128)(2,1)}, u32[]{:S(2)}) copy-start(bf16[256,3072]{1,0:T(8,128)(2,1)} %get-tuple-element.59.refs_0_.refs_3_.refs_6_.refs_9_) | copy-start | bytes 4718596
  107.4 20.8 %copy-start.3 = (f32[64,3072]{1,0:T(8,128)S(1)}, f32[64,3072]{1,0:T(8,128)}, u32[]{:S(2)}) copy-start(f32[64,3072]{1,0:T(8,128)} %get-tuple-element.67.a_ref) | copy-start | bytes 2359300
  107.4 15.5 %collective-permute-start.8 = (bf16[64,3072]{1,0:T(8,128)(2,1)}, bf16[64,3072]{1,0:T(8,128)(2,1)S(1)}, u32[]{:S(2)}, u32[]{:S(2)}) collective-permute-start(bf16[64,3072]{1,0:T(8,128)(2,1)} %get-tuple-element.71), channel_id=1, source_target_pairs={{0,2},{1,3},{2,0},{3,1},{4,6},{5,7},{6,4},{7,5},{8,10},{9,11},{10,... | collective-permute-start | bytes 1179656 | tf_op jit(solution)/shard_map/ppermute | solution.py:269
  109.3 18.9 %collective-permute-start.9 = (bf16[64,3072]{1,0:T(8,128)(2,1)}, bf16[64,3072]{1,0:T(8,128)(2,1)S(1)}, u32[]{:S(2)}, u32[]{:S(2)}) collective-permute-start(bf16[64,3072]{1,0:T(8,128)(2,1)} %get-tuple-element.72), channel_id=1, source_target_pairs={{0,1},{1,2},{2,3},{3,0},{4,5},{5,6},{6,7},{7,4},{8,9},{9,10},{10,1... | collective-permute-start | bytes 1179656 | tf_op jit(solution)/shard_map/ppermute | solution.py:269
  110.0 18.2 %collective-permute-start.10 = (bf16[64,3072]{1,0:T(8,128)(2,1)}, bf16[64,3072]{1,0:T(8,128)(2,1)S(1)}, u32[]{:S(2)}, u32[]{:S(2)}) collective-permute-start(bf16[64,3072]{1,0:T(8,128)(2,1)} %get-tuple-element.73), channel_id=1, source_target_pairs={{0,3},{1,0},{2,1},{3,2},{4,7},{5,4},{6,5},{7,6},{8,11},{9,8},{10,9... | collective-permute-start | bytes 1179656 | tf_op jit(solution)/shard_map/ppermute | solution.py:269
  122.5 10.3 %collective-permute-start.26 = (bf16[64,3072]{1,0:T(8,128)(2,1)}, bf16[64,3072]{1,0:T(8,128)(2,1)S(1)}, u32[]{:S(2)}, u32[]{:S(2)}) collective-permute-start(bf16[64,3072]{1,0:T(8,128)(2,1)} %get-tuple-element.95), channel_id=1, source_target_pairs={{0,8},{1,9},{2,10},{3,11},{4,12},{5,13},{6,14},{7,15},{8,0},{9,1},... | collective-permute-start | bytes 1179656 | tf_op jit(solution)/shard_map/ppermute | solution.py:269
  122.9 13.3 %collective-permute-start.27 = (bf16[64,3072]{1,0:T(8,128)(2,1)}, bf16[64,3072]{1,0:T(8,128)(2,1)S(1)}, u32[]{:S(2)}, u32[]{:S(2)}) collective-permute-start(bf16[64,3072]{1,0:T(8,128)(2,1)} %get-tuple-element.96), channel_id=1, source_target_pairs={{0,4},{1,5},{2,6},{3,7},{4,8},{5,9},{6,10},{7,11},{8,12},{9,13},{1... | collective-permute-start | bytes 1179656 | tf_op jit(solution)/shard_map/ppermute | solution.py:269
  122.9 13.3 %collective-permute-start.28 = (bf16[64,3072]{1,0:T(8,128)(2,1)}, bf16[64,3072]{1,0:T(8,128)(2,1)S(1)}, u32[]{:S(2)}, u32[]{:S(2)}) collective-permute-start(bf16[64,3072]{1,0:T(8,128)(2,1)} %get-tuple-element.97), channel_id=1, source_target_pairs={{0,12},{1,13},{2,14},{3,15},{4,0},{5,1},{6,2},{7,3},{8,4},{9,5},{1... | collective-permute-start | bytes 1179656 | tf_op jit(solution)/shard_map/ppermute | solution.py:269
  128.9 13.7 %collective-permute-start.11 = (bf16[64,3072]{1,0:T(8,128)(2,1)S(1)}, bf16[64,3072]{1,0:T(8,128)(2,1)S(1)}, u32[]{:S(2)}, u32[]{:S(2)}) collective-permute-start(bf16[64,3072]{1,0:T(8,128)(2,1)S(1)} %get-tuple-element.77.mine_ref), channel_id=1, source_target_pairs={{0,2},{1,3},{2,0},{3,1},{4,6},{5,7},{6,4},{7,5},{8,10},{9,11},{10,... | collective-permute-start | bytes 1179656 | tf_op jit(solution)/shard_map/ppermute | solution.py:269
  130.7 18.6 %collective-permute-start.12 = (bf16[64,3072]{1,0:T(8,128)(2,1)S(1)}, bf16[64,3072]{1,0:T(8,128)(2,1)S(1)}, u32[]{:S(2)}, u32[]{:S(2)}) collective-permute-start(bf16[64,3072]{1,0:T(8,128)(2,1)S(1)} %get-tuple-element.77.mine_ref), channel_id=1, source_target_pairs={{0,1},{1,2},{2,3},{3,0},{4,5},{5,6},{6,7},{7,4},{8,9},{9,10},{10,1... | collective-permute-start | bytes 1179656 | tf_op jit(solution)/shard_map/ppermute | solution.py:269
  132.8 16.5 %collective-permute-start.13 = (bf16[64,3072]{1,0:T(8,128)(2,1)S(1)}, bf16[64,3072]{1,0:T(8,128)(2,1)S(1)}, u32[]{:S(2)}, u32[]{:S(2)}) collective-permute-start(bf16[64,3072]{1,0:T(8,128)(2,1)S(1)} %get-tuple-element.77.mine_ref), channel_id=1, source_target_pairs={{0,3},{1,0},{2,1},{3,2},{4,7},{5,4},{6,5},{7,6},{8,11},{9,8},{10,9... | collective-permute-start | bytes 1179656 | tf_op jit(solution)/shard_map/ppermute | solution.py:269
  136.2 1.1 copy-start.2
  138.4 15.9 %collective-permute-start.29 = (bf16[64,3072]{1,0:T(8,128)(2,1)S(1)}, bf16[64,3072]{1,0:T(8,128)(2,1)S(1)}, u32[]{:S(2)}, u32[]{:S(2)}) collective-permute-start(bf16[64,3072]{1,0:T(8,128)(2,1)S(1)} %slope.1.mine_ref), channel_id=1, source_target_pairs={{0,8},{1,9},{2,10},{3,11},{4,12},{5,13},{6,14},{7,15},{8,0},{9,1},... | collective-permute-start | bytes 1179656 | tf_op jit(solution)/shard_map/ppermute | solution.py:269
  138.9 16.1 %collective-permute-start.30 = (bf16[64,3072]{1,0:T(8,128)(2,1)S(1)}, bf16[64,3072]{1,0:T(8,128)(2,1)S(1)}, u32[]{:S(2)}, u32[]{:S(2)}) collective-permute-start(bf16[64,3072]{1,0:T(8,128)(2,1)S(1)} %slope.1.mine_ref), channel_id=1, source_target_pairs={{0,4},{1,5},{2,6},{3,7},{4,8},{5,9},{6,10},{7,11},{8,12},{9,13},{1... | collective-permute-start | bytes 1179656 | tf_op jit(solution)/shard_map/ppermute | solution.py:269
  142.6 12.9 %collective-permute-start.31 = (bf16[64,3072]{1,0:T(8,128)(2,1)S(1)}, bf16[64,3072]{1,0:T(8,128)(2,1)S(1)}, u32[]{:S(2)}, u32[]{:S(2)}) collective-permute-start(bf16[64,3072]{1,0:T(8,128)(2,1)S(1)} %slope.1.mine_ref), channel_id=1, source_target_pairs={{0,12},{1,13},{2,14},{3,15},{4,0},{5,1},{6,2},{7,3},{8,4},{9,5},{1... | collective-permute-start | bytes 1179656 | tf_op jit(solution)/shard_map/ppermute | solution.py:269
  151.1 37.8 %collective-permute-start.14 = (bf16[256,3072]{1,0:T(8,128)(2,1)}, bf16[256,3072]{1,0:T(8,128)(2,1)}, u32[]{:S(2)}, u32[]{:S(2)}) collective-permute-start(bf16[256,3072]{1,0:T(8,128)(2,1)} %in_order.2), channel_id=1, source_target_pairs={{0,4},{1,5},{2,6},{3,7},{4,8},{5,9},{6,10},{7,11},{8,12},{9,13},{1... | collective-permute-start | bytes 4718600 | tf_op jit(solution)/shard_map/ppermute | solution.py:269
  151.1 39.0 %collective-permute-start.15 = (bf16[256,3072]{1,0:T(8,128)(2,1)}, bf16[256,3072]{1,0:T(8,128)(2,1)}, u32[]{:S(2)}, u32[]{:S(2)}) collective-permute-start(bf16[256,3072]{1,0:T(8,128)(2,1)} %in_order.2), channel_id=1, source_target_pairs={{0,12},{1,13},{2,14},{3,15},{4,0},{5,1},{6,2},{7,3},{8,4},{9,5},{1... | collective-permute-start | bytes 4718600 | tf_op jit(solution)/shard_map/ppermute | solution.py:269
  157.3 37.3 %collective-permute-start.32 = (bf16[256,3072]{1,0:T(8,128)(2,1)}, bf16[256,3072]{1,0:T(8,128)(2,1)}, u32[]{:S(2)}, u32[]{:S(2)}) collective-permute-start(bf16[256,3072]{1,0:T(8,128)(2,1)} %in_order.3), channel_id=1, source_target_pairs={{0,1},{1,2},{2,3},{3,0},{4,5},{5,6},{6,7},{7,4},{8,9},{9,10},{10,1... | collective-permute-start | bytes 4718600 | tf_op jit(solution)/shard_map/ppermute | solution.py:269
  157.9 37.9 %collective-permute-start.33 = (bf16[256,3072]{1,0:T(8,128)(2,1)}, bf16[256,3072]{1,0:T(8,128)(2,1)}, u32[]{:S(2)}, u32[]{:S(2)}) collective-permute-start(bf16[256,3072]{1,0:T(8,128)(2,1)} %in_order.3), channel_id=1, source_target_pairs={{0,3},{1,0},{2,1},{3,2},{4,7},{5,4},{6,5},{7,6},{8,11},{9,8},{10,9... | collective-permute-start | bytes 4718600 | tf_op jit(solution)/shard_map/ppermute | solution.py:269
  165.8 3.2 %slice-start = ((s8[4718592]{0:T(1024)(128)(4,1)}), s8[4194304]{0:T(1024)(128)(4,1)S(1)}, s32[]{:S(2)}) async-start(s8[4718592]{0:T(1024)(128)(4,1)} %bitcast.70), calls=%async_computation | async-start | bytes 8388608
  166.0 3.1 %slice-start.1 = ((s8[4718592]{0:T(1024)(128)(4,1)}), s8[524288]{0:T(1024)(128)(4,1)S(1)}, s32[]{:S(2)}) async-start(s8[4718592]{0:T(1024)(128)(4,1)} %bitcast.70), calls=%async_computation.1 | async-start | bytes 1048576
  191.3 19.9 %collective-permute-start.16 = (bf16[128,3072]{1,0:T(8,128)(2,1)S(1)}, bf16[128,3072]{1,0:T(8,128)(2,1)S(1)}, u32[]{:S(2)}, u32[]{:S(2)}) collective-permute-start(bf16[128,3072]{1,0:T(8,128)(2,1)S(1)} %slice.45), channel_id=1, source_target_pairs={{0,4},{1,5},{2,6},{3,7},{4,8},{5,9},{6,10},{7,11},{8,12},{9,13},{1... | collective-permute-start | bytes 2359304 | tf_op jit(solution)/shard_map/ppermute | solution.py:269
  191.4 20.7 %collective-permute-start.17 = (bf16[128,3072]{1,0:T(8,128)(2,1)S(1)}, bf16[128,3072]{1,0:T(8,128)(2,1)S(1)}, u32[]{:S(2)}, u32[]{:S(2)}) collective-permute-start(bf16[128,3072]{1,0:T(8,128)(2,1)S(1)} %slice.46), channel_id=1, source_target_pairs={{0,12},{1,13},{2,14},{3,15},{4,0},{5,1},{6,2},{7,3},{8,4},{9,5},{1... | collective-permute-start | bytes 2359304 | tf_op jit(solution)/shard_map/ppermute | solution.py:269
  197.0 19.7 %collective-permute-start.34 = (bf16[128,3072]{1,0:T(8,128)(2,1)S(1)}, bf16[128,3072]{1,0:T(8,128)(2,1)S(1)}, u32[]{:S(2)}, u32[]{:S(2)}) collective-permute-start(bf16[128,3072]{1,0:T(8,128)(2,1)S(1)} %slice.53), channel_id=1, source_target_pairs={{0,1},{1,2},{2,3},{3,0},{4,5},{5,6},{6,7},{7,4},{8,9},{9,10},{10,1... | collective-permute-start | bytes 2359304 | tf_op jit(solution)/shard_map/ppermute | solution.py:269
  197.9 18.9 %collective-permute-start.35 = (bf16[128,3072]{1,0:T(8,128)(2,1)S(1)}, bf16[128,3072]{1,0:T(8,128)(2,1)S(1)}, u32[]{:S(2)}, u32[]{:S(2)}) collective-permute-start(bf16[128,3072]{1,0:T(8,128)(2,1)S(1)} %slice.54), channel_id=1, source_target_pairs={{0,3},{1,0},{2,1},{3,2},{4,7},{5,4},{6,5},{7,6},{8,11},{9,8},{10,9... | collective-permute-start | bytes 2359304 | tf_op jit(solution)/shard_map/ppermute | solution.py:269
  213.0 3.9 %collective-permute-start.18 = (bf16[512,768]{1,0:T(8,128)(2,1)S(1)}, bf16[512,768]{1,0:T(8,128)(2,1)S(1)}, u32[]{:S(2)}, u32[]{:S(2)}) collective-permute-start(bf16[512,768]{1,0:T(8,128)(2,1)S(1)} %bitcast.76), channel_id=1, source_target_pairs={{0,16},{16,0},{32,48},{48,32},{64,80},{80,64},{96,112},{112,96},{1... | collective-permute-start | bytes 2359304 | tf_op jit(solution)/shard_map/ppermute | solution.py:269
  217.2 12.1 %collective-permute-start.21 = (bf16[128,768]{1,0:T(8,128)(2,1)S(1)}, bf16[128,768]{1,0:T(8,128)(2,1)S(1)}, u32[]{:S(2)}, u32[]{:S(2)}) collective-permute-start(bf16[128,768]{1,0:T(8,128)(2,1)S(1)} %get-tuple-element.84), channel_id=1, source_target_pairs={{0,96},{16,112},{32,0},{48,16},{64,32},{80,48},{96,64},{112,80},{1... | collective-permute-start | bytes 589832 | tf_op jit(solution)/shard_map/ppermute | solution.py:269
  219.5 10.6 %collective-permute-start.20 = (bf16[128,768]{1,0:T(8,128)(2,1)S(1)}, bf16[128,768]{1,0:T(8,128)(2,1)S(1)}, u32[]{:S(2)}, u32[]{:S(2)}) collective-permute-start(bf16[128,768]{1,0:T(8,128)(2,1)S(1)} %get-tuple-element.83), channel_id=1, source_target_pairs={{0,32},{16,48},{32,64},{48,80},{64,96},{80,112},{96,0},{112,16},{1... | collective-permute-start | bytes 589832 | tf_op jit(solution)/shard_map/ppermute | solution.py:269
  219.5 10.6 %collective-permute-start.19 = (bf16[128,768]{1,0:T(8,128)(2,1)S(1)}, bf16[128,768]{1,0:T(8,128)(2,1)S(1)}, u32[]{:S(2)}, u32[]{:S(2)}) collective-permute-start(bf16[128,768]{1,0:T(8,128)(2,1)S(1)} %get-tuple-element.82), channel_id=1, source_target_pairs={{0,64},{16,80},{32,96},{48,112},{64,0},{80,16},{96,32},{112,48},{1... | collective-permute-start | bytes 589832 | tf_op jit(solution)/shard_map/ppermute | solution.py:269
